TPU v7x, 512 devices: a whole 4x4x16 slice. The times are simulated.
512 devices in a mesh: mp: 32 (over z, y_lo), dp: 16 (over x, y_hi, core).
Axes of the slice: x: 4, y: 4 (y_hi: 2, y_lo: 2; y = y_hi * 2 + y_lo), z: 16, core: 2. Of those that a mesh axis runs over, the one named last changes fastest.
Arguments:
- inputs: bfloat16 [256, 8192], P('mp', 'dp'), may hold values from -6 to 6
- w_up: bfloat16 [8192, 32768], P('dp', 'mp'), may hold values from -0.0625 to 0.0625
- w_down: bfloat16 [32768, 8192], P('mp', 'dp'), may hold values from -0.03125 to 0.03125
- cotangent: bfloat16 [256, 8192], P('mp', 'dp'), may hold values from -6 to 6
Outputs:
- output: bfloat16 [256, 8192], P('mp', 'dp')
- grad_inputs: bfloat16 [256, 8192], P('mp', 'dp')
- grad_up: bfloat16 [8192, 32768], P('dp', 'mp')
- grad_down: bfloat16 [32768, 8192], P('mp', 'dp')
All inputs are finite; a program needn't handle non-finite values.
Results may differ from a plain program's by a relative error of at most 0.0049.
Values may be sent and summed in bfloat16 or wider, within the bound.
No kernel may reach another device: no remote copies, remote signals or barrier semaphores. Data moves between devices by JAX's collectives and lax.ppermute only.
A program may use at most 64 MiB of HBM per device.

v0:
```python
import jax
import jax.numpy as jnp
from jax import lax
from jax.sharding import PartitionSpec as P


def gelu_tanh(values):
    return (
        0.5
        * values
        * (1.0 + jnp.tanh(0.7978845608 * (values + 0.044715 * values * values * values)))
    )


def gelu_back(hidden, grad_act):
    unused, pullback = jax.vjp(gelu_tanh, hidden)
    return pullback(grad_act)[0].astype(jnp.bfloat16)


def local(inputs, w_up, w_down, cotangent):
    full_inputs = lax.all_gather(inputs, "mp", axis=0, tiled=True)
    partial_value = jnp.dot(full_inputs, w_up, preferred_element_type=jnp.float32)
    hidden = lax.psum(partial_value, "dp")
    activated = gelu_tanh(hidden).astype(jnp.bfloat16)
    taken = activated
    output = lax.psum_scatter(
        jnp.dot(taken, w_down, preferred_element_type=jnp.float32),
        "mp",
        scatter_dimension=0,
        tiled=True,
    ).astype(jnp.bfloat16)
    incoming = lax.all_gather(cotangent, "mp", axis=0, tiled=True)
    product = lax.dot_general(
        incoming, w_down, (((1,), (1,)), ((), ())), preferred_element_type=jnp.float32
    )
    back_hidden = product
    grad_sum_down = lax.dot_general(
        activated, incoming, (((0,), (0,)), ((), ())), preferred_element_type=jnp.float32
    )
    back_hidden, grad_sum_down = (back_hidden, grad_sum_down)
    grad_down = grad_sum_down.astype(jnp.bfloat16)
    grad_act = lax.psum(back_hidden, "dp")
    grad_hidden = gelu_back(hidden, grad_act)
    grad_up = lax.dot_general(
        full_inputs, grad_hidden, (((0,), (0,)), ((), ())), preferred_element_type=jnp.float32
    ).astype(jnp.bfloat16)
    taken = grad_hidden
    grad_inputs = lax.psum_scatter(
        lax.dot_general(taken, w_up, (((1,), (1,)), ((), ())), preferred_element_type=jnp.float32),
        "mp",
        scatter_dimension=0,
        tiled=True,
    ).astype(jnp.bfloat16)
    return (output, grad_inputs, grad_up, grad_down)


def solution(mesh):
    in_specs = (P("mp", "dp"), P("dp", "mp"), P("mp", "dp"), P("mp", "dp"))
    out_specs = (P("mp", "dp"), P("mp", "dp"), P("dp", "mp"), P("mp", "dp"))
    return jax.shard_map(local, mesh=mesh, in_specs=in_specs, out_specs=out_specs, check_vma=False)
```

profile of v0, /device:TPU:6, one launch (start us, length us, event | category | flops | bytes accessed | tf_op | source)
XLA Modules:
  0.0 582.1 jit_solution(4208164725356933076)
XLA Ops:
  7.2 0.0 copy-start
  7.2 0.0 all-reduce.3.cloned.1.call-start
  7.2 70.7 %all_gather.6 = bf16[256,512]{1,0:T(8,128)(2,1)S(1)} all-gather(bf16[8,512]{1,0:T(8,128)(2,1)} %param.4), channel_id=1, replica_groups=mesh['mp'=32,'dp'=16] {'mp'}, dimensions={0}, use_global_device_ids=true | all-gather | bytes 270336 | tf_op jit(solution)/shard_map/all_gather | solution.py:21
  78.0 60.1 %all_gather.7 = bf16[256,512]{1,0:T(8,128)(2,1)S(1)} all-gather(bf16[8,512]{1,0:T(8,128)(2,1)} %param.7), channel_id=1, replica_groups=mesh['mp'=32,'dp'=16] {'mp'}, dimensions={0}, use_global_device_ids=true | all-gather | bytes 270336 | tf_op jit(solution)/shard_map/all_gather | solution.py:32
  138.1 2.7 fusion.9
  140.7 0.0 copy-done
  140.7 1.4 fusion.8
  142.1 0.0 all-reduce.3.cloned.1.call-update
  142.2 0.0 reduce-scatter.5.cloned.1.call-start
  142.2 149.3 %all-reduce.3.cloned.1.call-done = (f32[256,1024]{1,0:T(8,128)}, f32[256,1024]{1,0:T(8,128)}) async-done(((f32[256,1024]{1,0:T(8,128)}, f32[256,1024]{1,0:T(8,128)}), (f32[256,1024]{1,0:T(8,128)}, f32[256,1024]{1,0:T(8,128)})) %all-reduce.3.cloned.1.call-update) | async-done | bytes 2097168 | tf_op jit(solution)/shard_map/psum | solution.py:23
  291.5 2.4 fusion.4
  293.9 0.0 copy-start.1
  293.9 1.3 fusion.10
  295.2 0.0 reduce-scatter.5.cloned.1.call-update
  295.2 0.0 reduce-scatter.3.cloned.1.call-start
  295.3 0.0 copy-done.1
  295.3 2.5 fusion.7
  297.8 0.0 reduce-scatter.3.cloned.1.call-update
  297.9 0.5 fusion
  298.3 1.3 copy.8
  299.6 2.8 convolution_convert_fusion
  302.4 135.9 %reduce-scatter.5.cloned.1.call-done = f32[8,512]{1,0:T(8,128)} async-done(((f32[256,512]{1,0:T(8,128)}), f32[8,512]{1,0:T(8,128)}) %reduce-scatter.5.cloned.1.call-update) | async-done | bytes 16400 | tf_op jit(solution)/shard_map/reduce_scatter | solution.py:48
  438.3 1.3 convert_element_type.24
  439.6 134.6 %reduce-scatter.3.cloned.1.call-done = f32[8,512]{1,0:T(8,128)} async-done(((f32[256,512]{1,0:T(8,128)}), f32[8,512]{1,0:T(8,128)}) %reduce-scatter.3.cloned.1.call-update) | async-done | bytes 16400 | tf_op jit(solution)/shard_map/reduce_scatter | solution.py:26
  574.2 1.3 convert_element_type.22
Async XLA Ops:
  7.2 133.6 %copy-start = (bf16[512,1024]{1,0:T(8,128)(2,1)S(1)}, bf16[512,1024]{1,0:T(8,128)(2,1)}, u32[]{:S(2)}) copy-start(bf16[512,1024]{1,0:T(8,128)(2,1)} %param.5) | copy-start | bytes 3145732
  7.2 284.4 %all-reduce.3.cloned.1.call-start = ((), (), s32[]{:S(2)}) async-start(), calls=%async_computation.4 | async-start | bytes 4194304 | tf_op jit(solution)/shard_map/psum | solution.py:23
  142.2 296.1 %reduce-scatter.5.cloned.1.call-start = ((), (), s32[]{:S(2)}) async-start(), calls=%async_computation.3 | async-start | bytes 540672 | tf_op jit(solution)/shard_map/reduce_scatter | solution.py:48
  293.9 1.3 copy-start.1
  295.2 279.0 %reduce-scatter.3.cloned.1.call-start = ((), (), s32[]{:S(2)}) async-start(), calls=%async_computation.2 | async-start | bytes 540672 | tf_op jit(solution)/shard_map/reduce_scatter | solution.py:26
Sparse Core Ops, SparseCore 0:
  142.3 149.2 all-reduce.2
  295.3 142.9 reduce-scatter.4
  441.3 132.8 reduce-scatter.2
where the time goes:
time: 582 us
  waiting for transfers between devices  420 us (72%)
  blocking collectives  131 us (23%)
  between operations  13.8 us (2%)
  matrix products  11.1 us (2%)
    psum x1, waiting for transfers between devices, local(): hidden = lax.psum(partial_value, 'dp')  149 us
    reduce_scatter x1, waiting for transfers between devices, local(): lax.psum_scatter(lax.dot_general(taken, w_up, (((1,), (1,)), ((), ())), p...  136 us
    reduce_scatter x1, waiting for transfers between devices, local(): lax.psum_scatter(jnp.dot(taken, w_down, preferred_element_type=jnp.float3...  135 us
    all_gather x1, blocking collectives, local(): full_inputs = lax.all_gather(inputs, 'mp', axis=0, tiled=True)  70.7 us
    all_gather x1, blocking collectives, local(): incoming = lax.all_gather(cotangent, 'mp', axis=0, tiled=True)  60.1 us
  transfers between devices with their start and end apart: 3, of which 3 were waited for; matrix products, arithmetic and copies ran while one was open for 1% of the time, Pallas kernels for 0%

commit v1 on v0

v1 whole, which is shorter than its diff:
```python
import jax
import jax.numpy as jnp
from jax import lax
from jax.sharding import Mesh
from jax.sharding import PartitionSpec as P

AXES = ("zh", "zl", "yl", "x", "yh", "core")
SIZES = (4, 4, 2, 4, 2, 2)
MP = ("zh", "zl", "yl")
DP = ("x", "yh", "core")
FAR = ("zh", "yl")
NEAR = "zl"
PLANE = ("x", "yh")
F32 = jnp.float32
BF16 = jnp.bfloat16


def gelu_tanh(values):
    return (
        0.5
        * values
        * (1.0 + jnp.tanh(0.7978845608 * (values + 0.044715 * values * values * values)))
    )


def gelu_back(hidden, grad_act):
    unused, pullback = jax.vjp(gelu_tanh, hidden)
    return pullback(grad_act)[0].astype(BF16)


def dot(a, b, ca, cb):
    return lax.dot_general(a, b, (((ca,), (cb,)), ((), ())), preferred_element_type=F32)


def spread(block, axes, count):
    copies = jnp.broadcast_to(block[None], (count,) + block.shape)
    return lax.all_to_all(copies, axes, 0, 0, tiled=True)


def swap(block):
    return lax.ppermute(block, "core", [(0, 1), (1, 0)])


def local(inputs, w_up, w_down, cotangent):
    core = lax.axis_index("core")
    pair = jnp.concatenate([inputs, cotangent], axis=1)
    far = spread(pair, FAR, 8).reshape(64, 1024)
    full = spread(far, NEAR, 4).reshape(256, 1024)
    mine = lax.dynamic_slice_in_dim(full, core * 128, 128, 0)
    other = lax.dynamic_slice_in_dim(full, (1 - core) * 128, 128, 0)

    def partials(rows):
        return jnp.concatenate(
            [
                dot(rows[:, :512], w_up, 1, 0).reshape(8, 16, 1024),
                dot(rows[:, 512:], w_down, 1, 1).reshape(8, 16, 1024),
            ],
            axis=1,
        )

    received = swap(partials(other))
    summed = (partials(mine) + received).astype(BF16)
    blocks = lax.all_to_all(summed, PLANE, 0, 0, tiled=True)
    total = jnp.sum(blocks.astype(F32), axis=0)
    hidden, grad_act = total[:16], total[16:]
    activated = gelu_tanh(hidden).astype(BF16)
    grad_hidden = gelu_back(hidden, grad_act)
    half = spread(jnp.concatenate([activated, grad_hidden], axis=0), PLANE, 8)
    half_other = swap(half)
    act = half[:, :16].reshape(128, 1024)
    grad = half[:, 16:].reshape(128, 1024)
    act_o = half_other[:, :16].reshape(128, 1024)
    grad_o = half_other[:, 16:].reshape(128, 1024)

    def outs(a, g):
        return jnp.concatenate([dot(a, w_down, 1, 0), dot(g, w_up, 1, 1)], axis=1).astype(BF16)

    out_mine = outs(act, grad)
    out_other = outs(act_o, grad_o)
    first = core == 0
    parts = jnp.concatenate(
        [jnp.where(first, out_mine, out_other), jnp.where(first, out_other, out_mine)], axis=0
    ).reshape(4, 64, 1024)
    near = jnp.sum(lax.all_to_all(parts, NEAR, 0, 0, tiled=True).astype(F32), axis=0)
    parts = near.astype(BF16).reshape(8, 8, 1024)
    sums = jnp.sum(lax.all_to_all(parts, FAR, 0, 0, tiled=True).astype(F32), axis=0).astype(BF16)

    both_a = jnp.concatenate([act, act_o], axis=0)
    both_g = jnp.concatenate([grad, grad_o], axis=0)
    rows = jnp.concatenate([mine, other], axis=0)
    grad_down = dot(both_a, rows[:, 512:], 0, 0).astype(BF16)
    grad_up = dot(rows[:, :512], both_g, 0, 0).astype(BF16)
    return (sums[:, :512], sums[:, 512:], grad_up, grad_down)


def solution(mesh):
    fine = Mesh(mesh.devices.reshape(SIZES), AXES)
    in_specs = (P(MP, DP), P(DP, MP), P(MP, DP), P(MP, DP))
    out_specs = (P(MP, DP), P(MP, DP), P(DP, MP), P(MP, DP))
    return jax.shard_map(local, mesh=fine, in_specs=in_specs, out_specs=out_specs, check_vma=False)
```

time: 582 us -> 133 us (0.23)
  waiting for transfers between devices: 420 us -> 35.4 us
  blocking collectives: 131 us -> 64.1 us
  starting transfers between devices: 0.12 us -> 18 us
  between operations: 13.8 us -> 0.84 us
    reduce_scatter x2 -> x0, waiting for transfers between devices: 270 us -> none  [the longest x1 136 us: local(): lax.psum_scatter(lax.dot_general(taken, w_up, (((1,), (1,)), ((), ())), p...]
    psum x1 -> x0, waiting for transfers between devices: 149 us -> none  [local(): hidden = lax.psum(partial_value, 'dp')]
    all_gather x2 -> x0, blocking collectives: 131 us -> none  [the longest x1 70.7 us: local(): full_inputs = lax.all_gather(inputs, 'mp', axis=0, tiled=True)]
    all_to_all x0 -> x3, blocking collectives: none -> 64.1 us  [the longest x1 30.3 us: spread(): return lax.all_to_all(copies, axes, 0, 0, tiled=True)]
    all_to_all x0 -> x3, waiting for transfers between devices: none -> 32.3 us  [the longest x2 20.8 us: spread(): return lax.all_to_all(copies, axes, 0, 0, tiled=True)]
    all_to_all x0 -> x3, starting transfers between devices: none -> 14.2 us  [the longest x2 9.12 us: spread(): return lax.all_to_all(copies, axes, 0, 0, tiled=True)]
  transfers between devices with their start and end apart: 3 -> 5, of which waited for: 3 -> 5; matrix products, arithmetic and copies ran while one was open for 1% -> 3% of each run, Pallas kernels for 0% -> 0%
where the time goes in v1:
time: 133 us; the launch traced here: 131 us
  blocking collectives  64.1 us (48%)
  waiting for transfers between devices  35.4 us (27%)
  starting transfers between devices  18 us (14%)
  matrix products  6.02 us (5%)
  other arithmetic  4.27 us (3%)
  local copies, waits for them, and re-layouts  2.46 us (2%)
    all_to_all x1, blocking collectives, spread(): return lax.all_to_all(copies, axes, 0, 0, tiled=True)  30.3 us
    all_to_all x2, waiting for transfers between devices, spread(): return lax.all_to_all(copies, axes, 0, 0, tiled=True)  20.8 us
    all_to_all x1, blocking collectives, local(): lax.all_to_all(parts, NEAR, 0, 0, tiled=True).astype(F32)  17.5 us
    all_to_all x1, blocking collectives, local(): blocks = lax.all_to_all(summed, PLANE, 0, 0, tiled=True)  16.2 us
    all_to_all x1, waiting for transfers between devices, local(): lax.all_to_all(parts, FAR, 0, 0, tiled=True).astype(F32)  11.4 us
    all_to_all x2, starting transfers between devices, spread(): return lax.all_to_all(copies, axes, 0, 0, tiled=True)  9.12 us
    dot_general x10, matrix products, dot(): lax.dot_general(a, b, (((ca,), (cb,)), ((), ())), preferred_element_type=...  6.02 us
    all_to_all x1, starting transfers between devices, local(): lax.all_to_all(parts, FAR, 0, 0, tiled=True).astype(F32)  5.08 us
  transfers between devices with their start and end apart: 5, of which 5 were waited for; matrix products, arithmetic and copies ran while one was open for 3% of the time, Pallas kernels for 0%

profile of v1, /device:TPU:6, one launch (start us, length us, event | category | flops | bytes accessed | tf_op | source)
XLA Modules:
  0.0 131.1 jit_solution(5299675007688530064)
XLA Ops:
  0.6 0.0 copy-start
  0.6 0.8 pad_maximum_fusion.7
  1.5 30.3 %all_to_all.30 = bf16[8,8,1024]{2,1,0:T(8,128)(2,1)S(1)} all-to-all(bf16[8,8,1024]{2,1,0:T(8,128)(2,1)S(1)} %broadcast_in_dim.8), channel_id=1, replica_groups=mesh['zh'=4,'zl'=4,'yl'=2,'x'=4,'yh'=2,'core'=2] {'zh','yl'}, dimensions={0} | all-to-all | bytes 262144 | tf_op jit(solution)/shard_map/all_to_all | solution.py:37
  31.8 0.9 broadcast_in_dim.10
  32.7 3.5 %all-to-all-start.1 = ((bf16[4,64,1024]{2,1,0:T(8,128)(2,1)}), bf16[4,64,1024]{2,1,0:T(8,128)(2,1)S(1)}, u32[]{:S(2)}, u32[]{:S(2)}) async-start(bf16[4,64,1024]{2,1,0:T(8,128)(2,1)} %broadcast_in_dim.10), calls=%async_computation.1 | async-start | bytes 1048576 | tf_op jit(solution)/shard_map/all_to_all | solution.py:37
  36.1 0.0 copy-start.1
  36.2 12.7 %all-to-all-done.1 = bf16[4,64,1024]{2,1,0:T(8,128)(2,1)S(1)} async-done(((bf16[4,64,1024]{2,1,0:T(8,128)(2,1)}), bf16[4,64,1024]{2,1,0:T(8,128)(2,1)S(1)}, u32[]{:S(2)}, u32[]{:S(2)}) %all-to-all-start.1) | async-done | bytes 524320 | tf_op jit(solution)/shard_map/all_to_all | solution.py:37
  48.8 0.0 copy-done
  48.8 0.3 fusion.12
  49.1 0.0 copy-done.1
  49.1 0.5 fusion.10
  49.6 1.0 pad_maximum_fusion
  50.7 1.9 %collective-permute-start = (f32[8,32,1024]{2,1,0:T(8,128)}, f32[8,32,1024]{2,1,0:T(8,128)}, u32[]{:S(2)}, u32[]{:S(2)}) collective-permute-start(f32[8,32,1024]{2,1,0:T(8,128)} %pad_maximum_fusion), channel_id=1, source_target_pairs={{0,1},{1,0},{2,3},{3,2},{4,5},{5,4},{6,7},{7,6},{8,9},{9,8},{10,11... | collective-permute-start | bytes 3145736 | tf_op jit(solution)/shard_map/ppermute | solution.py:41
  52.6 0.5 fusion.14
  53.1 0.3 fusion.16
  53.4 2.2 %collective-permute-done = f32[8,32,1024]{2,1,0:T(8,128)} collective-permute-done((f32[8,32,1024]{2,1,0:T(8,128)}, f32[8,32,1024]{2,1,0:T(8,128)}, u32[]{:S(2)}, u32[]{:S(2)}) %collective-permute-start) | collective-permute-done | bytes 1048608 | tf_op jit(solution)/shard_map/ppermute | solution.py:41
  55.5 1.4 %fusion = bf16[8,32,1024]{2,1,0:T(8,128)(2,1)S(1)} fusion(f32[8,32,1024]{2,1,0:T(8,128)} %collective-permute-done, f32[8,16,1024]{2,1,0:T(8,128)S(1)} %bitcast.29, f32[8,16,1024]{2,1,0:T(8,128)S(1)} %bitcast.30), kind=kLoop, calls=%fused_computation.7 | loop fusion | flops 786432 | bytes 2621440 | tf_op jit(solution)/shard_map/convert_element_type | solution.py:62
  56.9 16.2 %all_to_all.31 = bf16[8,32,1024]{2,1,0:T(8,128)(2,1)S(1)} all-to-all(bf16[8,32,1024]{2,1,0:T(8,128)(2,1)S(1)} %fusion), channel_id=1, replica_groups=mesh['zh'=4,'zl'=4,'yl'=2,'x'=4,'yh'=2,'core'=2] {'x','yh'}, dimensions={0} | all-to-all | bytes 1048576 | tf_op jit(solution)/shard_map/all_to_all | solution.py:63
  73.2 0.1 convert_reduce_fusion
  73.2 0.1 multiply_convert_fusion
  73.3 0.9 broadcast_in_dim.22
  74.2 5.6 %all-to-all-start.3 = ((bf16[8,32,1024]{2,1,0:T(8,128)(2,1)}), bf16[8,32,1024]{2,1,0:T(8,128)(2,1)S(1)}, u32[]{:S(2)}, u32[]{:S(2)}) async-start(bf16[8,32,1024]{2,1,0:T(8,128)(2,1)} %broadcast_in_dim.22), calls=%async_computation.3 | async-start | bytes 1048576 | tf_op jit(solution)/shard_map/all_to_all | solution.py:37
  79.8 8.2 %all-to-all-done.3 = bf16[8,32,1024]{2,1,0:T(8,128)(2,1)S(1)} async-done(((bf16[8,32,1024]{2,1,0:T(8,128)(2,1)}), bf16[8,32,1024]{2,1,0:T(8,128)(2,1)S(1)}, u32[]{:S(2)}, u32[]{:S(2)}) %all-to-all-start.3) | async-done | bytes 524320 | tf_op jit(solution)/shard_map/all_to_all | solution.py:37
  88.0 1.9 %collective-permute-start.1 = (bf16[8,32,1024]{2,1,0:T(8,128)(2,1)S(1)}, bf16[8,32,1024]{2,1,0:T(8,128)(2,1)S(1)}, u32[]{:S(2)}, u32[]{:S(2)}) collective-permute-start(bf16[8,32,1024]{2,1,0:T(8,128)(2,1)S(1)} %all-to-all-done.3), channel_id=1, source_target_pairs={{0,1},{1,0},{2,3},{3,2},{4,5},{5,4},{6,7},{7,6},{8,9},{9,8},{10,11... | collective-permute-start | bytes 1572872 | tf_op jit(solution)/shard_map/ppermute | solution.py:41
  90.0 0.0 copy-start.2
  90.0 0.5 convolution_convert_fusion.4
  90.5 0.3 convolution_convert_fusion.5
  90.8 0.0 copy-done.2
  90.8 1.0 collective-permute-done.1
  91.9 0.5 convolution_convert_fusion.2
  92.4 0.3 convolution_convert_fusion.3
  92.7 0.1 broadcast_select_fusion.1
  92.8 17.5 %all_to_all.32 = bf16[4,64,1024]{2,1,0:T(8,128)(2,1)S(1)} all-to-all(bf16[4,64,1024]{2,1,0:T(8,128)(2,1)S(1)} %bitcast.31), channel_id=1, replica_groups=mesh['zh'=4,'zl'=4,'yl'=2,'x'=4,'yh'=2,'core'=2] {'zl'}, dimensions={0} | all-to-all | bytes 1048576 | tf_op jit(solution)/shard_map/all_to_all | solution.py:84
  110.3 0.0 copy-start.3
  110.3 0.7 reduce_sum.34
  111.0 5.1 %all-to-all-start.5 = ((bf16[8,8,1024]{2,1,0:T(8,128)(2,1)}), bf16[8,8,1024]{2,1,0:T(8,128)(2,1)S(1)}, u32[]{:S(2)}, u32[]{:S(2)}) async-start(bf16[8,8,1024]{2,1,0:T(8,128)(2,1)} %bitcast.11), calls=%async_computation.5 | async-start | bytes 262144 | tf_op jit(solution)/shard_map/all_to_all | solution.py:86
  116.1 0.0 copy-done.3
  116.2 1.4 %convolution_convert_fusion.1 = bf16[512,1024]{1,0:T(8,128)(2,1)} fusion(bf16[128,1024]{1,0:T(8,128)(2,1)S(1)} %bitcast.41, bf16[128,1024]{1,0:T(8,128)(2,1)S(1)} %bitcast.37, bf16[128,1024]{1,0:T(8,128)(2,1)S(1)} %get-tuple-element.5, bf16[128,1024]{1,0:T(8,128)(2,1)S(1)} %get-tuple-element.4), kind=kOutput, calls=%fused_computation.1 | convolution fusion | flops 270532608 | bytes 2097152 | tf_op jit(solution)/shard_map/dot_general | solution.py:32
  117.6 1.4 %convolution_convert_fusion = bf16[1024,512]{1,0:T(8,128)(2,1)} fusion(bf16[128,1024]{1,0:T(8,128)(2,1)S(1)} %bitcast.39, bf16[128,1024]{1,0:T(8,128)(2,1)S(1)} %bitcast.35, bf16[128,1024]{1,0:T(8,128)(2,1)S(1)} %get-tuple-element.4, bf16[128,1024]{1,0:T(8,128)(2,1)S(1)} %get-tuple-element.5), kind=kOutput, calls=%fused_computation | convolution fusion | flops 270532608 | bytes 2097152 | tf_op jit(solution)/shard_map/dot_general | solution.py:32
  119.0 11.4 %all-to-all-done.5 = bf16[8,8,1024]{2,1,0:T(8,128)(2,1)S(1)} async-done(((bf16[8,8,1024]{2,1,0:T(8,128)(2,1)}), bf16[8,8,1024]{2,1,0:T(8,128)(2,1)S(1)}, u32[]{:S(2)}, u32[]{:S(2)}) %all-to-all-start.5) | async-done | bytes 131104 | tf_op jit(solution)/shard_map/all_to_all | solution.py:86
  130.5 0.6 fusion.30
  (7 shorter events, 0.2 us)
Async XLA Ops:
  0.6 48.2 %copy-start = (bf16[512,1024]{1,0:T(8,128)(2,1)S(1)}, bf16[512,1024]{1,0:T(8,128)(2,1)}, u32[]{:S(2)}) copy-start(bf16[512,1024]{1,0:T(8,128)(2,1)} %param.5) | copy-start | bytes 3145732
  32.7 16.2 %all-to-all-start.1 = ((bf16[4,64,1024]{2,1,0:T(8,128)(2,1)}), bf16[4,64,1024]{2,1,0:T(8,128)(2,1)S(1)}, u32[]{:S(2)}, u32[]{:S(2)}) async-start(bf16[4,64,1024]{2,1,0:T(8,128)(2,1)} %broadcast_in_dim.10), calls=%async_computation.1 | async-start | bytes 1048576 | tf_op jit(solution)/shard_map/all_to_all | solution.py:37
  36.1 13.0 %copy-start.1 = (bf16[1024,512]{1,0:T(8,128)(2,1)S(1)}, bf16[1024,512]{1,0:T(8,128)(2,1)}, u32[]{:S(2)}) copy-start(bf16[1024,512]{1,0:T(8,128)(2,1)} %param.6) | copy-start | bytes 3145732
  50.7 4.9 %collective-permute-start = (f32[8,32,1024]{2,1,0:T(8,128)}, f32[8,32,1024]{2,1,0:T(8,128)}, u32[]{:S(2)}, u32[]{:S(2)}) collective-permute-start(f32[8,32,1024]{2,1,0:T(8,128)} %pad_maximum_fusion), channel_id=1, source_target_pairs={{0,1},{1,0},{2,3},{3,2},{4,5},{5,4},{6,7},{7,6},{8,9},{9,8},{10,11... | collective-permute-start | bytes 3145736 | tf_op jit(solution)/shard_map/ppermute | solution.py:41
  74.2 13.8 %all-to-all-start.3 = ((bf16[8,32,1024]{2,1,0:T(8,128)(2,1)}), bf16[8,32,1024]{2,1,0:T(8,128)(2,1)S(1)}, u32[]{:S(2)}, u32[]{:S(2)}) async-start(bf16[8,32,1024]{2,1,0:T(8,128)(2,1)} %broadcast_in_dim.22), calls=%async_computation.3 | async-start | bytes 1048576 | tf_op jit(solution)/shard_map/all_to_all | solution.py:37
  88.0 3.8 %collective-permute-start.1 = (bf16[8,32,1024]{2,1,0:T(8,128)(2,1)S(1)}, bf16[8,32,1024]{2,1,0:T(8,128)(2,1)S(1)}, u32[]{:S(2)}, u32[]{:S(2)}) collective-permute-start(bf16[8,32,1024]{2,1,0:T(8,128)(2,1)S(1)} %all-to-all-done.3), channel_id=1, source_target_pairs={{0,1},{1,0},{2,3},{3,2},{4,5},{5,4},{6,7},{7,6},{8,9},{9,8},{10,11... | collective-permute-start | bytes 1572872 | tf_op jit(solution)/shard_map/ppermute | solution.py:41
  90.0 0.8 copy-start.2
  110.3 5.9 %copy-start.3 = (bf16[8,16,1024]{2,1,0:T(8,128)(2,1)S(1)}, bf16[8,16,1024]{2,1,0:T(8,128)(2,1)}, u32[]{:S(2)}) copy-start(bf16[8,16,1024]{2,1,0:T(8,128)(2,1)} %copy-done.2) | copy-start | bytes 786436
  111.0 19.4 %all-to-all-start.5 = ((bf16[8,8,1024]{2,1,0:T(8,128)(2,1)}), bf16[8,8,1024]{2,1,0:T(8,128)(2,1)S(1)}, u32[]{:S(2)}, u32[]{:S(2)}) async-start(bf16[8,8,1024]{2,1,0:T(8,128)(2,1)} %bitcast.11), calls=%async_computation.5 | async-start | bytes 262144 | tf_op jit(solution)/shard_map/all_to_all | solution.py:86

commit v2 on v1

--- a/solution.py
+++ b/solution.py
@@ -4,12 +4,12 @@
 from jax.sharding import Mesh
 from jax.sharding import PartitionSpec as P
 
-AXES = ("zh", "zl", "yl", "x", "yh", "core")
-SIZES = (4, 4, 2, 4, 2, 2)
-MP = ("zh", "zl", "yl")
+AXES = ("zf", "zn", "yl", "x", "yh", "core")
+SIZES = (8, 2, 2, 4, 2, 2)
+MP = ("zf", "zn", "yl")
 DP = ("x", "yh", "core")
-FAR = ("zh", "yl")
-NEAR = "zl"
+FAR = "zf"
+NEAR = ("zn", "yl")
 PLANE = ("x", "yh")
 F32 = jnp.float32
 BF16 = jnp.bfloat16
@@ -37,6 +37,13 @@
     return lax.all_to_all(copies, axes, 0, 0, tiled=True)
 
 
+def total(blocks):
+    acc = blocks[0].astype(F32)
+    for i in range(1, blocks.shape[0]):
+        acc = acc + blocks[i].astype(F32)
+    return acc
+
+
 def swap(block):
     return lax.ppermute(block, "core", [(0, 1), (1, 0)])
 
@@ -58,11 +65,10 @@
             axis=1,
         )
 
-    received = swap(partials(other))
+    received = swap(partials(other).astype(BF16))
     summed = (partials(mine) + received).astype(BF16)
     blocks = lax.all_to_all(summed, PLANE, 0, 0, tiled=True)
-    total = jnp.sum(blocks.astype(F32), axis=0)
-    hidden, grad_act = total[:16], total[16:]
+    hidden, grad_act = total(blocks[:, :16]), total(blocks[:, 16:])
     activated = gelu_tanh(hidden).astype(BF16)
     grad_hidden = gelu_back(hidden, grad_act)
     half = spread(jnp.concatenate([activated, grad_hidden], axis=0), PLANE, 8)
@@ -81,9 +87,9 @@
     parts = jnp.concatenate(
         [jnp.where(first, out_mine, out_other), jnp.where(first, out_other, out_mine)], axis=0
     ).reshape(4, 64, 1024)
-    near = jnp.sum(lax.all_to_all(parts, NEAR, 0, 0, tiled=True).astype(F32), axis=0)
+    near = total(lax.all_to_all(parts, NEAR, 0, 0, tiled=True))
     parts = near.astype(BF16).reshape(8, 8, 1024)
-    sums = jnp.sum(lax.all_to_all(parts, FAR, 0, 0, tiled=True).astype(F32), axis=0).astype(BF16)
+    sums = total(lax.all_to_all(parts, FAR, 0, 0, tiled=True)).astype(BF16)
 
     both_a = jnp.concatenate([act, act_o], axis=0)
     both_g = jnp.concatenate([grad, grad_o], axis=0)

time: 133 us -> 117 us (0.88)
  waiting for transfers between devices: 35.4 us -> 29.5 us
  blocking collectives: 64.1 us -> 58.9 us
  other arithmetic: 4.27 us -> 2.04 us
  starting transfers between devices: 18 us -> 16.4 us
    all_to_all x2, waiting for transfers between devices: 20.8 us -> 14.7 us  [spread(): return lax.all_to_all(copies, axes, 0, 0, tiled=True)]
    all_to_all x1, blocking collectives: 17.5 us -> 11.5 us  [local(): near = total(lax.all_to_all(parts, NEAR, 0, 0, tiled=True))]
    all_to_all x1, starting transfers between devices: 5.08 us -> 3.37 us  [local(): sums = total(lax.all_to_all(parts, FAR, 0, 0, tiled=True)).astype(BF16)]
  transfers between devices with their start and end apart: 5 -> 5, of which waited for: 5 -> 5; matrix products, arithmetic and copies ran while one was open for 3% -> 4% of each run, Pallas kernels for 0% -> 0%
where the time goes in v2:
time: 117 us; the launch traced here: 116 us
  blocking collectives  58.9 us (50%)
  waiting for transfers between devices  29.5 us (25%)
  starting transfers between devices  16.4 us (14%)
  matrix products  6.04 us (5%)
  local copies, waits for them, and re-layouts  2.47 us (2%)
  other arithmetic  2.04 us (2%)
    all_to_all x1, blocking collectives, spread(): return lax.all_to_all(copies, axes, 0, 0, tiled=True)  30.9 us
    all_to_all x1, blocking collectives, local(): blocks = lax.all_to_all(summed, PLANE, 0, 0, tiled=True)  16.5 us
    all_to_all x2, waiting for transfers between devices, spread(): return lax.all_to_all(copies, axes, 0, 0, tiled=True)  14.7 us
    all_to_all x1, waiting for transfers between devices, local(): sums = total(lax.all_to_all(parts, FAR, 0, 0, tiled=True)).astype(BF16)  12.7 us
    all_to_all x1, blocking collectives, local(): near = total(lax.all_to_all(parts, NEAR, 0, 0, tiled=True))  11.5 us
    all_to_all x2, starting transfers between devices, spread(): return lax.all_to_all(copies, axes, 0, 0, tiled=True)  9.25 us
    dot_general x10, matrix products, dot(): lax.dot_general(a, b, (((ca,), (cb,)), ((), ())), preferred_element_type=...  6.04 us
    ppermute x2, starting transfers between devices, swap(): return lax.ppermute(block, 'core', [(0, 1), (1, 0)])  3.83 us
  transfers between devices with their start and end apart: 5, of which 5 were waited for; matrix products, arithmetic and copies ran while one was open for 4% of the time, Pallas kernels for 0%

profile of v2, /device:TPU:6, one launch (start us, length us, event | category | flops | bytes accessed | tf_op | source)
XLA Modules:
  0.0 116.2 jit_solution(2540777258584957062)
XLA Ops:
  0.6 0.0 copy-start
  0.6 0.8 pad_maximum_fusion.7
  1.5 30.9 %all_to_all.30 = bf16[8,8,1024]{2,1,0:T(8,128)(2,1)S(1)} all-to-all(bf16[8,8,1024]{2,1,0:T(8,128)(2,1)S(1)} %broadcast_in_dim.8), channel_id=1, replica_groups=mesh['zf'=8,'zn'=2,'yl'=2,'x'=4,'yh'=2,'core'=2] {'zf'}, dimensions={0} | all-to-all | bytes 262144 | tf_op jit(solution)/shard_map/all_to_all | solution.py:37
  32.3 0.9 broadcast_in_dim.10
  33.2 0.0 copy-start.1
  33.2 3.6 %all-to-all-start.1 = ((bf16[4,64,1024]{2,1,0:T(8,128)(2,1)}), bf16[4,64,1024]{2,1,0:T(8,128)(2,1)S(1)}, u32[]{:S(2)}, u32[]{:S(2)}) async-start(bf16[4,64,1024]{2,1,0:T(8,128)(2,1)} %broadcast_in_dim.10), calls=%async_computation.1 | async-start | bytes 1048576 | tf_op jit(solution)/shard_map/all_to_all | solution.py:37
  36.8 6.5 %all-to-all-done.1 = bf16[4,64,1024]{2,1,0:T(8,128)(2,1)S(1)} async-done(((bf16[4,64,1024]{2,1,0:T(8,128)(2,1)}), bf16[4,64,1024]{2,1,0:T(8,128)(2,1)S(1)}, u32[]{:S(2)}, u32[]{:S(2)}) %all-to-all-start.1) | async-done | bytes 524320 | tf_op jit(solution)/shard_map/all_to_all | solution.py:37
  43.4 0.0 copy-done
  43.4 0.3 convolution_convert_fusion.3
  43.7 0.0 copy-done.1
  43.7 0.5 convolution_convert_fusion.2
  44.2 1.9 %collective-permute-start = (bf16[8,32,1024]{2,1,0:T(8,128)(2,1)S(1)}, bf16[8,32,1024]{2,1,0:T(8,128)(2,1)S(1)}, u32[]{:S(2)}, u32[]{:S(2)}) collective-permute-start(bf16[8,32,1024]{2,1,0:T(8,128)(2,1)S(1)} %pad_maximum_fusion), channel_id=1, source_target_pairs={{0,1},{1,0},{2,3},{3,2},{4,5},{5,4},{6,7},{7,6},{8,9},{9,8},{10,11... | collective-permute-start | bytes 1572872 | tf_op jit(solution)/shard_map/ppermute | solution.py:48
  46.1 0.5 fusion.13
  46.6 0.3 fusion.15
  46.9 1.1 collective-permute-done
  48.0 0.1 fusion
  48.2 16.5 %all_to_all.31 = bf16[8,32,1024]{2,1,0:T(8,128)(2,1)S(1)} all-to-all(bf16[8,32,1024]{2,1,0:T(8,128)(2,1)S(1)} %fusion), channel_id=1, replica_groups=mesh['zf'=8,'zn'=2,'yl'=2,'x'=4,'yh'=2,'core'=2] {'x','yh'}, dimensions={0} | all-to-all | bytes 1048576 | tf_op jit(solution)/shard_map/all_to_all | solution.py:70
  64.7 0.1 multiply_convert_fusion
  64.8 0.1 fusion.20
  64.9 0.9 broadcast_in_dim.22
  65.7 5.6 %all-to-all-start.3 = ((bf16[8,32,1024]{2,1,0:T(8,128)(2,1)}), bf16[8,32,1024]{2,1,0:T(8,128)(2,1)S(1)}, u32[]{:S(2)}, u32[]{:S(2)}) async-start(bf16[8,32,1024]{2,1,0:T(8,128)(2,1)} %broadcast_in_dim.22), calls=%async_computation.3 | async-start | bytes 1048576 | tf_op jit(solution)/shard_map/all_to_all | solution.py:37
  71.4 8.2 %all-to-all-done.3 = bf16[8,32,1024]{2,1,0:T(8,128)(2,1)S(1)} async-done(((bf16[8,32,1024]{2,1,0:T(8,128)(2,1)}), bf16[8,32,1024]{2,1,0:T(8,128)(2,1)S(1)}, u32[]{:S(2)}, u32[]{:S(2)}) %all-to-all-start.3) | async-done | bytes 524320 | tf_op jit(solution)/shard_map/all_to_all | solution.py:37
  79.6 1.9 %collective-permute-start.1 = (bf16[8,32,1024]{2,1,0:T(8,128)(2,1)S(1)}, bf16[8,32,1024]{2,1,0:T(8,128)(2,1)S(1)}, u32[]{:S(2)}, u32[]{:S(2)}) collective-permute-start(bf16[8,32,1024]{2,1,0:T(8,128)(2,1)S(1)} %all-to-all-done.3), channel_id=1, source_target_pairs={{0,1},{1,0},{2,3},{3,2},{4,5},{5,4},{6,7},{7,6},{8,9},{9,8},{10,11... | collective-permute-start | bytes 1572872 | tf_op jit(solution)/shard_map/ppermute | solution.py:48
  81.5 0.0 copy-start.2
  81.5 0.5 convolution_convert_fusion.6
  82.0 0.3 convolution_convert_fusion.7
  82.3 0.0 copy-done.2
  82.4 1.0 collective-permute-done.1
  83.4 0.5 convolution_convert_fusion.4
  83.9 0.3 convolution_convert_fusion.5
  84.2 0.1 broadcast_select_fusion.1
  84.4 11.5 %all_to_all.32 = bf16[4,64,1024]{2,1,0:T(8,128)(2,1)S(1)} all-to-all(bf16[4,64,1024]{2,1,0:T(8,128)(2,1)S(1)} %bitcast.68), channel_id=1, replica_groups=mesh['zf'=8,'zn'=2,'yl'=2,'x'=4,'yh'=2,'core'=2] {'zn','yl'}, dimensions={0} | all-to-all | bytes 1048576 | tf_op jit(solution)/shard_map/all_to_all | solution.py:90
  95.9 0.0 copy-start.3
  95.9 0.7 fusion.10
  96.6 3.4 %all-to-all-start.5 = ((bf16[8,8,1024]{2,1,0:T(8,128)(2,1)}), bf16[8,8,1024]{2,1,0:T(8,128)(2,1)S(1)}, u32[]{:S(2)}, u32[]{:S(2)}) async-start(bf16[8,8,1024]{2,1,0:T(8,128)(2,1)} %fusion.10), calls=%async_computation.5 | async-start | bytes 262144 | tf_op jit(solution)/shard_map/all_to_all | solution.py:92
  100.0 0.0 copy-done.3
  100.0 1.4 %convolution_convert_fusion = bf16[1024,512]{1,0:T(8,128)(2,1)} fusion(bf16[128,1024]{1,0:T(8,128)(2,1)S(1)} %bitcast.78, bf16[128,1024]{1,0:T(8,128)(2,1)S(1)} %bitcast.74, bf16[128,1024]{1,0:T(8,128)(2,1)S(1)} %get-tuple-element.6, bf16[128,1024]{1,0:T(8,128)(2,1)S(1)} %get-tuple-element.7), kind=kOutput, calls=%fused_computation | convolution fusion | flops 270532608 | bytes 2097152 | tf_op jit(solution)/shard_map/dot_general | solution.py:32
  101.5 1.4 %convolution_convert_fusion.1 = bf16[512,1024]{1,0:T(8,128)(2,1)} fusion(bf16[128,1024]{1,0:T(8,128)(2,1)S(1)} %bitcast.76, bf16[128,1024]{1,0:T(8,128)(2,1)S(1)} %bitcast.72, bf16[128,1024]{1,0:T(8,128)(2,1)S(1)} %get-tuple-element.7, bf16[128,1024]{1,0:T(8,128)(2,1)S(1)} %get-tuple-element.6), kind=kOutput, calls=%fused_computation.1 | convolution fusion | flops 270532608 | bytes 2097152 | tf_op jit(solution)/shard_map/dot_general | solution.py:32
  102.9 12.7 %all-to-all-done.5 = bf16[8,8,1024]{2,1,0:T(8,128)(2,1)S(1)} async-done(((bf16[8,8,1024]{2,1,0:T(8,128)(2,1)}), bf16[8,8,1024]{2,1,0:T(8,128)(2,1)S(1)}, u32[]{:S(2)}, u32[]{:S(2)}) %all-to-all-start.5) | async-done | bytes 131104 | tf_op jit(solution)/shard_map/all_to_all | solution.py:92
  115.6 0.6 fusion.34
  (8 shorter events, 0.2 us)
Async XLA Ops:
  0.6 42.7 %copy-start = (bf16[512,1024]{1,0:T(8,128)(2,1)S(1)}, bf16[512,1024]{1,0:T(8,128)(2,1)}, u32[]{:S(2)}) copy-start(bf16[512,1024]{1,0:T(8,128)(2,1)} %param.5) | copy-start | bytes 3145732
  33.2 10.5 %copy-start.1 = (bf16[1024,512]{1,0:T(8,128)(2,1)S(1)}, bf16[1024,512]{1,0:T(8,128)(2,1)}, u32[]{:S(2)}) copy-start(bf16[1024,512]{1,0:T(8,128)(2,1)} %param.6) | copy-start | bytes 3145732
  33.2 10.2 %all-to-all-start.1 = ((bf16[4,64,1024]{2,1,0:T(8,128)(2,1)}), bf16[4,64,1024]{2,1,0:T(8,128)(2,1)S(1)}, u32[]{:S(2)}, u32[]{:S(2)}) async-start(bf16[4,64,1024]{2,1,0:T(8,128)(2,1)} %broadcast_in_dim.10), calls=%async_computation.1 | async-start | bytes 1048576 | tf_op jit(solution)/shard_map/all_to_all | solution.py:37
  44.2 3.8 %collective-permute-start = (bf16[8,32,1024]{2,1,0:T(8,128)(2,1)S(1)}, bf16[8,32,1024]{2,1,0:T(8,128)(2,1)S(1)}, u32[]{:S(2)}, u32[]{:S(2)}) collective-permute-start(bf16[8,32,1024]{2,1,0:T(8,128)(2,1)S(1)} %pad_maximum_fusion), channel_id=1, source_target_pairs={{0,1},{1,0},{2,3},{3,2},{4,5},{5,4},{6,7},{7,6},{8,9},{9,8},{10,11... | collective-permute-start | bytes 1572872 | tf_op jit(solution)/shard_map/ppermute | solution.py:48
  65.7 13.8 %all-to-all-start.3 = ((bf16[8,32,1024]{2,1,0:T(8,128)(2,1)}), bf16[8,32,1024]{2,1,0:T(8,128)(2,1)S(1)}, u32[]{:S(2)}, u32[]{:S(2)}) async-start(bf16[8,32,1024]{2,1,0:T(8,128)(2,1)} %broadcast_in_dim.22), calls=%async_computation.3 | async-start | bytes 1048576 | tf_op jit(solution)/shard_map/all_to_all | solution.py:37
  79.6 3.8 %collective-permute-start.1 = (bf16[8,32,1024]{2,1,0:T(8,128)(2,1)S(1)}, bf16[8,32,1024]{2,1,0:T(8,128)(2,1)S(1)}, u32[]{:S(2)}, u32[]{:S(2)}) collective-permute-start(bf16[8,32,1024]{2,1,0:T(8,128)(2,1)S(1)} %all-to-all-done.3), channel_id=1, source_target_pairs={{0,1},{1,0},{2,3},{3,2},{4,5},{5,4},{6,7},{7,6},{8,9},{9,8},{10,11... | collective-permute-start | bytes 1572872 | tf_op jit(solution)/shard_map/ppermute | solution.py:48
  81.5 0.8 copy-start.2
  95.9 4.2 %copy-start.3 = (bf16[8,16,1024]{2,1,0:T(8,128)(2,1)S(1)}, bf16[8,16,1024]{2,1,0:T(8,128)(2,1)}, u32[]{:S(2)}) copy-start(bf16[8,16,1024]{2,1,0:T(8,128)(2,1)} %copy-done.2) | copy-start | bytes 786436
  96.6 19.0 %all-to-all-start.5 = ((bf16[8,8,1024]{2,1,0:T(8,128)(2,1)}), bf16[8,8,1024]{2,1,0:T(8,128)(2,1)S(1)}, u32[]{:S(2)}, u32[]{:S(2)}) async-start(bf16[8,8,1024]{2,1,0:T(8,128)(2,1)} %fusion.10), calls=%async_computation.5 | async-start | bytes 262144 | tf_op jit(solution)/shard_map/all_to_all | solution.py:92

commit v3 on v2

--- a/solution.py
+++ b/solution.py
@@ -11,6 +11,7 @@
 FAR = "zf"
 NEAR = ("zn", "yl")
 PLANE = ("x", "yh")
+ORDER = (5, 6, 7, 0, 1, 2, 3, 4)
 F32 = jnp.float32
 BF16 = jnp.bfloat16
 
@@ -32,9 +33,12 @@
     return lax.dot_general(a, b, (((ca,), (cb,)), ((), ())), preferred_element_type=F32)
 
 
-def spread(block, axes, count):
-    copies = jnp.broadcast_to(block[None], (count,) + block.shape)
-    return lax.all_to_all(copies, axes, 0, 0, tiled=True)
+def trade(chunks, axes, order=None):
+    return lax.all_to_all(chunks, axes, 0, 0, axis_index_groups=order, tiled=True)
+
+
+def spread(block, axes, count, order=None):
+    return trade(jnp.broadcast_to(block[None], (count,) + block.shape), axes, order)
 
 
 def total(blocks):
@@ -51,7 +55,7 @@
 def local(inputs, w_up, w_down, cotangent):
     core = lax.axis_index("core")
     pair = jnp.concatenate([inputs, cotangent], axis=1)
-    far = spread(pair, FAR, 8).reshape(64, 1024)
+    far = spread(pair, FAR, 8, [ORDER]).reshape(64, 1024)
     full = spread(far, NEAR, 4).reshape(256, 1024)
     mine = lax.dynamic_slice_in_dim(full, core * 128, 128, 0)
     other = lax.dynamic_slice_in_dim(full, (1 - core) * 128, 128, 0)
@@ -67,7 +71,7 @@
 
     received = swap(partials(other).astype(BF16))
     summed = (partials(mine) + received).astype(BF16)
-    blocks = lax.all_to_all(summed, PLANE, 0, 0, tiled=True)
+    blocks = trade(summed, PLANE)
     hidden, grad_act = total(blocks[:, :16]), total(blocks[:, 16:])
     activated = gelu_tanh(hidden).astype(BF16)
     grad_hidden = gelu_back(hidden, grad_act)
@@ -87,9 +91,9 @@
     parts = jnp.concatenate(
         [jnp.where(first, out_mine, out_other), jnp.where(first, out_other, out_mine)], axis=0
     ).reshape(4, 64, 1024)
-    near = total(lax.all_to_all(parts, NEAR, 0, 0, tiled=True))
+    near = total(trade(parts, NEAR))
     parts = near.astype(BF16).reshape(8, 8, 1024)
-    sums = total(lax.all_to_all(parts, FAR, 0, 0, tiled=True)).astype(BF16)
+    sums = total(trade(parts, FAR, [ORDER])).astype(BF16)
 
     both_a = jnp.concatenate([act, act_o], axis=0)
     both_g = jnp.concatenate([grad, grad_o], axis=0)

time: 117 us -> 111 us (0.949)
  waiting for transfers between devices: 29.5 us -> 21.1 us
  starting transfers between devices: 16.4 us -> 24.2 us
  blocking collectives: 58.9 us -> 52.5 us
    all_to_all x3, waiting for transfers between devices: 27.4 us -> 19.1 us  [trade(): lax.all_to_all(chunks, axes, 0, 0, axis_index_groups=order, tiled=True)]
    all_to_all x3, starting transfers between devices: 12.6 us -> 20.4 us  [trade(): lax.all_to_all(chunks, axes, 0, 0, axis_index_groups=order, tiled=True)]
    all_to_all x3, blocking collectives: 58.9 us -> 52.5 us  [trade(): lax.all_to_all(chunks, axes, 0, 0, axis_index_groups=order, tiled=True)]
where the time goes in v3:
time: 111 us; the launch traced here: 109 us
  blocking collectives  52.5 us (47%)
  starting transfers between devices  24.2 us (22%)
  waiting for transfers between devices  21.1 us (19%)
  matrix products  6.03 us (5%)
  local copies, waits for them, and re-layouts  2.46 us (2%)
  other arithmetic  2.04 us (2%)
    all_to_all x3, blocking collectives, trade(): lax.all_to_all(chunks, axes, 0, 0, axis_index_groups=order, tiled=True)  52.5 us
    all_to_all x3, starting transfers between devices, trade(): lax.all_to_all(chunks, axes, 0, 0, axis_index_groups=order, tiled=True)  20.4 us
    all_to_all x3, waiting for transfers between devices, trade(): lax.all_to_all(chunks, axes, 0, 0, axis_index_groups=order, tiled=True)  19.1 us
    dot_general x10, matrix products, dot(): lax.dot_general(a, b, (((ca,), (cb,)), ((), ())), preferred_element_type=...  6.03 us
    ppermute x2, starting transfers between devices, swap(): return lax.ppermute(block, 'core', [(0, 1), (1, 0)])  3.83 us
  transfers between devices with their start and end apart: 5, of which 5 were waited for; matrix products, arithmetic and copies ran while one was open for 4% of the time, Pallas kernels for 0%

profile of v3, /device:TPU:6, one launch (start us, length us, event | category | flops | bytes accessed | tf_op | source)
XLA Modules:
  0.0 109.2 jit_solution(10690216151089169316)
XLA Ops:
  0.6 0.0 copy-start
  0.6 0.8 pad_maximum_fusion.7
  1.5 24.5 %all_to_all.30 = bf16[8,8,1024]{2,1,0:T(8,128)(2,1)S(1)} all-to-all(bf16[8,8,1024]{2,1,0:T(8,128)(2,1)S(1)} %broadcast_in_dim.8), channel_id=1, replica_groups={{320,384,448,0,64,128,192,256},{321,385,449,1,65,129,193,257},{322,386,..., dimensions={0} | all-to-all | bytes 262144 | tf_op jit(solution)/shard_map/all_to_all | solution.py:37
  26.0 0.9 broadcast_in_dim.10
  26.8 0.0 copy-start.1
  26.8 3.6 %all-to-all-start.1 = ((bf16[4,64,1024]{2,1,0:T(8,128)(2,1)}), bf16[4,64,1024]{2,1,0:T(8,128)(2,1)S(1)}, u32[]{:S(2)}, u32[]{:S(2)}) async-start(bf16[4,64,1024]{2,1,0:T(8,128)(2,1)} %broadcast_in_dim.10), calls=%async_computation.1 | async-start | bytes 1048576 | tf_op jit(solution)/shard_map/all_to_all | solution.py:37
  30.5 6.5 %all-to-all-done.1 = bf16[4,64,1024]{2,1,0:T(8,128)(2,1)S(1)} async-done(((bf16[4,64,1024]{2,1,0:T(8,128)(2,1)}), bf16[4,64,1024]{2,1,0:T(8,128)(2,1)S(1)}, u32[]{:S(2)}, u32[]{:S(2)}) %all-to-all-start.1) | async-done | bytes 524320 | tf_op jit(solution)/shard_map/all_to_all | solution.py:37
  37.0 0.0 copy-done
  37.0 0.3 convolution_convert_fusion.3
  37.3 0.0 copy-done.1
  37.3 0.5 convolution_convert_fusion.2
  37.9 1.9 %collective-permute-start = (bf16[8,32,1024]{2,1,0:T(8,128)(2,1)S(1)}, bf16[8,32,1024]{2,1,0:T(8,128)(2,1)S(1)}, u32[]{:S(2)}, u32[]{:S(2)}) collective-permute-start(bf16[8,32,1024]{2,1,0:T(8,128)(2,1)S(1)} %pad_maximum_fusion), channel_id=1, source_target_pairs={{0,1},{1,0},{2,3},{3,2},{4,5},{5,4},{6,7},{7,6},{8,9},{9,8},{10,11... | collective-permute-start | bytes 1572872 | tf_op jit(solution)/shard_map/ppermute | solution.py:52
  39.8 0.5 fusion.13
  40.3 0.3 fusion.15
  40.6 1.1 collective-permute-done
  41.7 0.1 fusion
  41.8 16.5 %all_to_all.31 = bf16[8,32,1024]{2,1,0:T(8,128)(2,1)S(1)} all-to-all(bf16[8,32,1024]{2,1,0:T(8,128)(2,1)S(1)} %fusion), channel_id=1, replica_groups=mesh['zf'=8,'zn'=2,'yl'=2,'x'=4,'yh'=2,'core'=2] {'x','yh'}, dimensions={0} | all-to-all | bytes 1048576 | tf_op jit(solution)/shard_map/all_to_all | solution.py:37
  58.3 0.1 multiply_convert_fusion
  58.4 0.1 fusion.20
  58.5 0.9 broadcast_in_dim.22
  59.4 5.6 %all-to-all-start.3 = ((bf16[8,32,1024]{2,1,0:T(8,128)(2,1)}), bf16[8,32,1024]{2,1,0:T(8,128)(2,1)S(1)}, u32[]{:S(2)}, u32[]{:S(2)}) async-start(bf16[8,32,1024]{2,1,0:T(8,128)(2,1)} %broadcast_in_dim.22), calls=%async_computation.3 | async-start | bytes 1048576 | tf_op jit(solution)/shard_map/all_to_all | solution.py:37
  65.0 8.2 %all-to-all-done.3 = bf16[8,32,1024]{2,1,0:T(8,128)(2,1)S(1)} async-done(((bf16[8,32,1024]{2,1,0:T(8,128)(2,1)}), bf16[8,32,1024]{2,1,0:T(8,128)(2,1)S(1)}, u32[]{:S(2)}, u32[]{:S(2)}) %all-to-all-start.3) | async-done | bytes 524320 | tf_op jit(solution)/shard_map/all_to_all | solution.py:37
  73.2 1.9 %collective-permute-start.1 = (bf16[8,32,1024]{2,1,0:T(8,128)(2,1)S(1)}, bf16[8,32,1024]{2,1,0:T(8,128)(2,1)S(1)}, u32[]{:S(2)}, u32[]{:S(2)}) collective-permute-start(bf16[8,32,1024]{2,1,0:T(8,128)(2,1)S(1)} %all-to-all-done.3), channel_id=1, source_target_pairs={{0,1},{1,0},{2,3},{3,2},{4,5},{5,4},{6,7},{7,6},{8,9},{9,8},{10,11... | collective-permute-start | bytes 1572872 | tf_op jit(solution)/shard_map/ppermute | solution.py:52
  75.2 0.0 copy-start.2
  75.2 0.5 convolution_convert_fusion.6
  75.7 0.3 convolution_convert_fusion.7
  76.0 0.0 copy-done.2
  76.0 1.0 collective-permute-done.1
  77.0 0.5 convolution_convert_fusion.4
  77.5 0.3 convolution_convert_fusion.5
  77.9 0.1 broadcast_select_fusion.1
  78.0 11.5 %all_to_all.32 = bf16[4,64,1024]{2,1,0:T(8,128)(2,1)S(1)} all-to-all(bf16[4,64,1024]{2,1,0:T(8,128)(2,1)S(1)} %bitcast.68), channel_id=1, replica_groups=mesh['zf'=8,'zn'=2,'yl'=2,'x'=4,'yh'=2,'core'=2] {'zn','yl'}, dimensions={0} | all-to-all | bytes 1048576 | tf_op jit(solution)/shard_map/all_to_all | solution.py:37
  89.5 0.0 copy-start.3
  89.5 0.7 fusion.10
  90.2 11.1 %all-to-all-start.5 = ((bf16[8,8,1024]{2,1,0:T(8,128)(2,1)}), bf16[8,8,1024]{2,1,0:T(8,128)(2,1)S(1)}, u32[]{:S(2)}, u32[]{:S(2)}) async-start(bf16[8,8,1024]{2,1,0:T(8,128)(2,1)} %fusion.10), calls=%async_computation.5 | async-start | bytes 262144 | tf_op jit(solution)/shard_map/all_to_all | solution.py:37
  101.4 0.0 copy-done.3
  101.4 1.4 %convolution_convert_fusion = bf16[1024,512]{1,0:T(8,128)(2,1)} fusion(bf16[128,1024]{1,0:T(8,128)(2,1)S(1)} %bitcast.78, bf16[128,1024]{1,0:T(8,128)(2,1)S(1)} %bitcast.74, bf16[128,1024]{1,0:T(8,128)(2,1)S(1)} %get-tuple-element.6, bf16[128,1024]{1,0:T(8,128)(2,1)S(1)} %get-tuple-element.7), kind=kOutput, calls=%fused_computation | convolution fusion | flops 270532608 | bytes 2097152 | tf_op jit(solution)/shard_map/dot_general | solution.py:33
  102.8 1.4 %convolution_convert_fusion.1 = bf16[512,1024]{1,0:T(8,128)(2,1)} fusion(bf16[128,1024]{1,0:T(8,128)(2,1)S(1)} %bitcast.76, bf16[128,1024]{1,0:T(8,128)(2,1)S(1)} %bitcast.72, bf16[128,1024]{1,0:T(8,128)(2,1)S(1)} %get-tuple-element.7, bf16[128,1024]{1,0:T(8,128)(2,1)S(1)} %get-tuple-element.6), kind=kOutput, calls=%fused_computation.1 | convolution fusion | flops 270532608 | bytes 2097152 | tf_op jit(solution)/shard_map/dot_general | solution.py:33
  104.3 4.3 %all-to-all-done.5 = bf16[8,8,1024]{2,1,0:T(8,128)(2,1)S(1)} async-done(((bf16[8,8,1024]{2,1,0:T(8,128)(2,1)}), bf16[8,8,1024]{2,1,0:T(8,128)(2,1)S(1)}, u32[]{:S(2)}, u32[]{:S(2)}) %all-to-all-start.5) | async-done | bytes 131104 | tf_op jit(solution)/shard_map/all_to_all | solution.py:37
  108.6 0.6 fusion.34
  (8 shorter events, 0.2 us)
Async XLA Ops:
  0.6 36.4 %copy-start = (bf16[512,1024]{1,0:T(8,128)(2,1)S(1)}, bf16[512,1024]{1,0:T(8,128)(2,1)}, u32[]{:S(2)}) copy-start(bf16[512,1024]{1,0:T(8,128)(2,1)} %param.5) | copy-start | bytes 3145732
  26.8 10.5 %copy-start.1 = (bf16[1024,512]{1,0:T(8,128)(2,1)S(1)}, bf16[1024,512]{1,0:T(8,128)(2,1)}, u32[]{:S(2)}) copy-start(bf16[1024,512]{1,0:T(8,128)(2,1)} %param.6) | copy-start | bytes 3145732
  26.8 10.2 %all-to-all-start.1 = ((bf16[4,64,1024]{2,1,0:T(8,128)(2,1)}), bf16[4,64,1024]{2,1,0:T(8,128)(2,1)S(1)}, u32[]{:S(2)}, u32[]{:S(2)}) async-start(bf16[4,64,1024]{2,1,0:T(8,128)(2,1)} %broadcast_in_dim.10), calls=%async_computation.1 | async-start | bytes 1048576 | tf_op jit(solution)/shard_map/all_to_all | solution.py:37
  37.9 3.8 %collective-permute-start = (bf16[8,32,1024]{2,1,0:T(8,128)(2,1)S(1)}, bf16[8,32,1024]{2,1,0:T(8,128)(2,1)S(1)}, u32[]{:S(2)}, u32[]{:S(2)}) collective-permute-start(bf16[8,32,1024]{2,1,0:T(8,128)(2,1)S(1)} %pad_maximum_fusion), channel_id=1, source_target_pairs={{0,1},{1,0},{2,3},{3,2},{4,5},{5,4},{6,7},{7,6},{8,9},{9,8},{10,11... | collective-permute-start | bytes 1572872 | tf_op jit(solution)/shard_map/ppermute | solution.py:52
  59.4 13.8 %all-to-all-start.3 = ((bf16[8,32,1024]{2,1,0:T(8,128)(2,1)}), bf16[8,32,1024]{2,1,0:T(8,128)(2,1)S(1)}, u32[]{:S(2)}, u32[]{:S(2)}) async-start(bf16[8,32,1024]{2,1,0:T(8,128)(2,1)} %broadcast_in_dim.22), calls=%async_computation.3 | async-start | bytes 1048576 | tf_op jit(solution)/shard_map/all_to_all | solution.py:37
  73.2 3.8 %collective-permute-start.1 = (bf16[8,32,1024]{2,1,0:T(8,128)(2,1)S(1)}, bf16[8,32,1024]{2,1,0:T(8,128)(2,1)S(1)}, u32[]{:S(2)}, u32[]{:S(2)}) collective-permute-start(bf16[8,32,1024]{2,1,0:T(8,128)(2,1)S(1)} %all-to-all-done.3), channel_id=1, source_target_pairs={{0,1},{1,0},{2,3},{3,2},{4,5},{5,4},{6,7},{7,6},{8,9},{9,8},{10,11... | collective-permute-start | bytes 1572872 | tf_op jit(solution)/shard_map/ppermute | solution.py:52
  75.2 0.8 copy-start.2
  89.5 11.9 %copy-start.3 = (bf16[8,16,1024]{2,1,0:T(8,128)(2,1)S(1)}, bf16[8,16,1024]{2,1,0:T(8,128)(2,1)}, u32[]{:S(2)}) copy-start(bf16[8,16,1024]{2,1,0:T(8,128)(2,1)} %copy-done.2) | copy-start | bytes 786436
  90.2 18.4 %all-to-all-start.5 = ((bf16[8,8,1024]{2,1,0:T(8,128)(2,1)}), bf16[8,8,1024]{2,1,0:T(8,128)(2,1)S(1)}, u32[]{:S(2)}, u32[]{:S(2)}) async-start(bf16[8,8,1024]{2,1,0:T(8,128)(2,1)} %fusion.10), calls=%async_computation.5 | async-start | bytes 262144 | tf_op jit(solution)/shard_map/all_to_all | solution.py:37

commit v4 on v3

v4 whole, which is shorter than its diff:
```python
import jax
import jax.numpy as jnp
from jax import lax
from jax.experimental import pallas as pl
from jax.experimental.pallas import tpu as pltpu
from jax.sharding import Mesh
from jax.sharding import PartitionSpec as P

AXES = ("zf", "zn", "yl", "x", "yh", "core")
SIZES = (8, 2, 2, 4, 2, 2)
MP = ("zf", "zn", "yl")
DP = ("x", "yh", "core")
FAR = "zf"
NEAR = ("zn", "yl")
PLANE = ("x", "yh")
ORDER = (5, 6, 7, 0, 1, 2, 3, 4)
F32 = jnp.float32
BF16 = jnp.bfloat16


def gelu_tanh(values):
    return (
        0.5
        * values
        * (1.0 + jnp.tanh(0.7978845608 * (values + 0.044715 * values * values * values)))
    )


def gelu_back(hidden, grad_act):
    unused, pullback = jax.vjp(gelu_tanh, hidden)
    return pullback(grad_act)[0].astype(BF16)


def dot(a, b, ca, cb):
    return lax.dot_general(a, b, (((ca,), (cb,)), ((), ())), preferred_element_type=F32)


def trade(chunks, axes, order=None):
    return lax.all_to_all(chunks, axes, 0, 0, axis_index_groups=order, tiled=True)


def spread(block, axes, count, order=None):
    return trade(jnp.broadcast_to(block[None], (count,) + block.shape), axes, order)


def total(blocks):
    acc = blocks[0].astype(F32)
    for i in range(1, blocks.shape[0]):
        acc = acc + blocks[i].astype(F32)
    return acc


def swap(block):
    return lax.ppermute(block, "core", [(0, 1), (1, 0)])


def call(body, shape, *args, dtype=BF16, after=()):
    shape = jax.tree.map(lambda s: pltpu.VMEM(s, dtype), shape, is_leaf=lambda s: isinstance(s[0], int))
    args = [pltpu.with_memory_space_constraint(a, pltpu.VMEM) for a in args]
    return pl.pallas_call(
        body,
        out_shape=shape,
        in_specs=[pl.BlockSpec(memory_space=pltpu.VMEM)] * len(args)
        + [pl.BlockSpec(memory_space=pl.ANY)] * len(after),
        out_specs=jax.tree.map(lambda s: pl.BlockSpec(memory_space=pltpu.VMEM), shape),
        compiler_params=pltpu.CompilerParams(vmem_limit_bytes=40 * 2**20),
    )(*args, *after)


def half_rows(ref, mine):
    core = lax.axis_index("core")
    start = pl.multiple_of((core if mine else 1 - core) * 128, 128)
    return ref[pl.ds(start, 128), :]


def partials(full, w_up, w_down, mine):
    rows = half_rows(full, mine)
    hidden = dot(rows[:, :512], w_up[...], 1, 0)
    grad_act = dot(rows[:, 512:], w_down[...], 1, 1)
    return hidden.reshape(8, 16, 1024), grad_act.reshape(8, 16, 1024)


def first_half(full, w_up, w_down, out):
    hidden, grad_act = partials(full, w_up, w_down, False)
    out[:, :16] = hidden.astype(BF16)
    out[:, 16:] = grad_act.astype(BF16)


def second_half(full, w_up, w_down, out):
    out[:, :16], out[:, 16:] = partials(full, w_up, w_down, True)


def add_received(mine, received, out):
    out[...] = (mine[...] + received[...].astype(F32)).astype(BF16)


def activate(blocks, out):
    hidden = total(blocks[:, :16])
    grad_act = total(blocks[:, 16:])
    cubic = 0.7978845608 * (hidden + 0.044715 * hidden * hidden * hidden)
    tanh = jnp.tanh(cubic)
    activated = (0.5 * hidden * (1.0 + tanh)).astype(BF16)
    slope = 0.7978845608 * (1.0 + 3 * 0.044715 * hidden * hidden)
    back = 0.5 * (1.0 + tanh) + 0.5 * hidden * (1.0 - tanh * tanh) * slope
    grad_hidden = (grad_act * back).astype(BF16)
    for i in range(8):
        out[i, :16] = activated
        out[i, 16:] = grad_hidden


def products(half, w_up, w_down):
    act = half[:, :16].reshape(128, 1024)
    grad = half[:, 16:].reshape(128, 1024)
    return dot(act, w_down[...], 1, 0).astype(BF16), dot(grad, w_up[...], 1, 1).astype(BF16)


def first_out(half, w_up, w_down, out):
    out[:, :512], out[:, 512:] = products(half, w_up, w_down)


def second_out(half, w_up, w_down, mine, out):
    core = lax.axis_index("core")
    other = pl.multiple_of((1 - core) * 128, 128)
    out[pl.ds(pl.multiple_of(core * 128, 128), 128), :] = mine[...]
    result, grad = products(half, w_up, w_down)
    out[pl.ds(other, 128), :512] = result
    out[pl.ds(other, 128), 512:] = grad


def add_four(blocks, out):
    out[...] = total(blocks).astype(BF16)


def repeat_four(block, out):
    for i in range(4):
        out[i] = block[...]


def align(full, half, half_other, after, act, grad, x, g):
    for i, part in enumerate((half, half_other)):
        act[128 * i : 128 * i + 128] = part[:, :16].reshape(128, 1024)
        grad[128 * i : 128 * i + 128] = part[:, 16:].reshape(128, 1024)
        rows = half_rows(full, i == 0)
        x[128 * i : 128 * i + 128] = rows[:, :512]
        g[128 * i : 128 * i + 128] = rows[:, 512:]


def local(inputs, w_up, w_down, cotangent):
    pair = jnp.concatenate([inputs, cotangent], axis=1)
    far = spread(pair, FAR, 8, [ORDER]).reshape(64, 1024)
    full = trade(call(repeat_four, (4, 64, 1024), far), NEAR).reshape(256, 1024)
    received = swap(call(first_half, (8, 32, 1024), full, w_up, w_down))
    own = call(second_half, (8, 32, 1024), full, w_up, w_down, dtype=F32)
    summed = call(add_received, (8, 32, 1024), own, received)
    half = trade(call(activate, (8, 32, 1024), trade(summed, PLANE)), PLANE)
    half_other = swap(half)
    mine = call(first_out, (128, 1024), half, w_up, w_down)
    parts = call(second_out, (256, 1024), half_other, w_up, w_down, mine).reshape(4, 64, 1024)
    near = call(add_four, (64, 1024), trade(parts, NEAR))
    sums = total(trade(near.reshape(8, 8, 1024), FAR, [ORDER])).astype(BF16)

    sizes = [(256, 1024), (256, 1024), (256, 512), (256, 512)]
    act, grad, x, g = call(align, sizes, full, half, half_other, after=(near,))
    grad_down = dot(act, g, 0, 0).astype(BF16)
    grad_up = dot(x, grad, 0, 0).astype(BF16)
    return (sums[:, :512], sums[:, 512:], grad_up, grad_down)


def solution(mesh):
    fine = Mesh(mesh.devices.reshape(SIZES), AXES)
    in_specs = (P(MP, DP), P(DP, MP), P(MP, DP), P(MP, DP))
    out_specs = (P(MP, DP), P(MP, DP), P(DP, MP), P(MP, DP))
    return jax.shard_map(local, mesh=fine, in_specs=in_specs, out_specs=out_specs, check_vma=False)
```

time: 111 us -> 109 us (0.982)
  blocking collectives: 52.5 us -> 75.9 us
  waiting for transfers between devices: 21.1 us -> 6.73 us
  starting transfers between devices: 24.2 us -> 15.5 us
  Pallas kernels: 0 us -> 3.61 us
  matrix products: 6.03 us -> 2.87 us
  local copies, waits for them, and re-layouts: 2.46 us -> 0.62 us
  other arithmetic: 2.04 us -> 0.74 us
    all_to_all x3 -> x5, blocking collectives: 52.5 us -> 75.9 us  [trade(): lax.all_to_all(chunks, axes, 0, 0, axis_index_groups=order, tiled=True)]
    all_to_all x3 -> x1, waiting for transfers between devices: 19.1 us -> 4.27 us  [trade(): lax.all_to_all(chunks, axes, 0, 0, axis_index_groups=order, tiled=True)]
    all_to_all x3 -> x1, starting transfers between devices: 20.4 us -> 11.7 us  [trade(): lax.all_to_all(chunks, axes, 0, 0, axis_index_groups=order, tiled=True)]
    pallas_call x0 -> x9, Pallas kernels: none -> 3.61 us  [call(): pl.pallas_call(body, out_shape=shape, in_specs=[pl.BlockSpec(memory_space...]
    dot_general x10 -> x2, matrix products: 6.03 us -> 2.87 us  [dot(): lax.dot_general(a, b, (((ca,), (cb,)), ((), ())), preferred_element_type=...]
    broadcast_in_dim x3 -> x1, local copies, waits for them, and re-layouts: 1.72 us -> 0.01 us  [spread(): jnp.broadcast_to(block[None], (count,) + block.shape)]
  transfers between devices with their start and end apart: 5 -> 3, of which waited for: 5 -> 3; matrix products, arithmetic and copies ran while one was open for 4% -> 3% of each run, Pallas kernels for 0% -> 1%
where the time goes in v4:
time: 109 us; the launch traced here: 107 us
  blocking collectives  75.9 us (70%)
  starting transfers between devices  15.5 us (14%)
  waiting for transfers between devices  6.73 us (6%)
  Pallas kernels  3.61 us (3%)
  matrix products  2.87 us (3%)
    all_to_all x5, blocking collectives, trade(): lax.all_to_all(chunks, axes, 0, 0, axis_index_groups=order, tiled=True)  75.9 us
    all_to_all x1, starting transfers between devices, trade(): lax.all_to_all(chunks, axes, 0, 0, axis_index_groups=order, tiled=True)  11.7 us
    all_to_all x1, waiting for transfers between devices, trade(): lax.all_to_all(chunks, axes, 0, 0, axis_index_groups=order, tiled=True)  4.27 us
    ppermute x2, starting transfers between devices, swap(): return lax.ppermute(block, 'core', [(0, 1), (1, 0)])  3.83 us
    pallas_call x9, Pallas kernels, call(): pl.pallas_call(body, out_shape=shape, in_specs=[pl.BlockSpec(memory_space...  3.61 us
    dot_general x2, matrix products, dot(): lax.dot_general(a, b, (((ca,), (cb,)), ((), ())), preferred_element_type=...  2.87 us
    ppermute x2, waiting for transfers between devices, swap(): return lax.ppermute(block, 'core', [(0, 1), (1, 0)])  2.46 us
  transfers between devices with their start and end apart: 3, of which 3 were waited for; matrix products, arithmetic and copies ran while one was open for 3% of the time, Pallas kernels for 1%

profile of v4, /device:TPU:6, one launch (start us, length us, event | category | flops | bytes accessed | tf_op | source)
XLA Modules:
  0.0 106.7 jit_solution(9487382085376981264)
XLA Ops:
  0.6 0.7 pad_maximum_fusion
  1.3 0.0 copy-start
  1.4 0.0 copy-start.1
  1.4 24.6 %all_to_all.30 = bf16[8,8,1024]{2,1,0:T(8,128)(2,1)S(1)} all-to-all(bf16[8,8,1024]{2,1,0:T(8,128)(2,1)S(1)} %broadcast_in_dim.2), channel_id=1, replica_groups={{320,384,448,0,64,128,192,256},{321,385,449,1,65,129,193,257},{322,386,..., dimensions={0} | all-to-all | bytes 262144 | tf_op jit(solution)/shard_map/all_to_all | solution.py:39
  26.1 9.8 %all_to_all.31 = bf16[4,64,1024]{2,1,0:T(8,128)(2,1)S(1)} all-to-all(bf16[4,64,1024]{2,1,0:T(8,128)(2,1)S(1)} %shard_map.75), channel_id=1, replica_groups=mesh['zf'=8,'zn'=2,'yl'=2,'x'=4,'yh'=2,'core'=2] {'zn','yl'}, dimensions={0} | all-to-all | bytes 1048576 | tf_op jit(solution)/shard_map/all_to_all | solution.py:39
  35.8 0.0 copy-done
  35.8 0.0 copy-done.1
  35.8 0.6 shard_map.77
  36.5 1.9 %collective-permute-start = (bf16[8,32,1024]{2,1,0:T(8,128)(2,1)S(1)}, bf16[8,32,1024]{2,1,0:T(8,128)(2,1)S(1)}, u32[]{:S(2)}, u32[]{:S(2)}) collective-permute-start(bf16[8,32,1024]{2,1,0:T(8,128)(2,1)S(1)} %shard_map.77), channel_id=1, source_target_pairs={{0,1},{1,0},{2,3},{3,2},{4,5},{5,4},{6,7},{7,6},{8,9},{9,8},{10,11... | collective-permute-start | bytes 1572872 | tf_op jit(solution)/shard_map/ppermute | solution.py:54
  38.4 0.6 shard_map.76.mine
  39.0 1.2 %collective-permute-done.received = bf16[8,32,1024]{2,1,0:T(8,128)(2,1)S(1)} collective-permute-done((bf16[8,32,1024]{2,1,0:T(8,128)(2,1)S(1)}, bf16[8,32,1024]{2,1,0:T(8,128)(2,1)S(1)}, u32[]{:S(2)}, u32[]{:S(2)}) %collective-permute-start) | collective-permute-done | bytes 524320 | tf_op jit(solution)/shard_map/ppermute | solution.py:54
  40.3 0.1 shard_map.78
  40.4 16.3 %all_to_all.32.blocks = bf16[8,32,1024]{2,1,0:T(8,128)(2,1)S(1)} all-to-all(bf16[8,32,1024]{2,1,0:T(8,128)(2,1)S(1)} %shard_map.78), channel_id=1, replica_groups=mesh['zf'=8,'zn'=2,'yl'=2,'x'=4,'yh'=2,'core'=2] {'x','yh'}, dimensions={0} | all-to-all | bytes 1048576 | tf_op jit(solution)/shard_map/all_to_all | solution.py:39
  56.7 0.1 shard_map.79
  56.8 13.7 %all_to_all.33.half = bf16[8,32,1024]{2,1,0:T(8,128)(2,1)S(1)} all-to-all(bf16[8,32,1024]{2,1,0:T(8,128)(2,1)S(1)} %shard_map.79), channel_id=1, replica_groups=mesh['zf'=8,'zn'=2,'yl'=2,'x'=4,'yh'=2,'core'=2] {'x','yh'}, dimensions={0} | all-to-all | bytes 1048576 | tf_op jit(solution)/shard_map/all_to_all | solution.py:39
  70.5 1.9 %collective-permute-start.1 = (bf16[8,32,1024]{2,1,0:T(8,128)(2,1)S(1)}, bf16[8,32,1024]{2,1,0:T(8,128)(2,1)S(1)}, u32[]{:S(2)}, u32[]{:S(2)}) collective-permute-start(bf16[8,32,1024]{2,1,0:T(8,128)(2,1)S(1)} %all_to_all.33.half), channel_id=1, source_target_pairs={{0,1},{1,0},{2,3},{3,2},{4,5},{5,4},{6,7},{7,6},{8,9},{9,8},{10,11... | collective-permute-start | bytes 1572872 | tf_op jit(solution)/shard_map/ppermute | solution.py:54
  72.4 0.6 shard_map.80.mine
  73.0 1.2 %collective-permute-done.1.half.half_other = bf16[8,32,1024]{2,1,0:T(8,128)(2,1)S(1)} collective-permute-done((bf16[8,32,1024]{2,1,0:T(8,128)(2,1)S(1)}, bf16[8,32,1024]{2,1,0:T(8,128)(2,1)S(1)}, u32[]{:S(2)}, u32[]{:S(2)}) %collective-permute-start.1) | collective-permute-done | bytes 524320 | tf_op jit(solution)/shard_map/ppermute | solution.py:54
  74.3 0.6 shard_map.81
  74.9 11.5 %all_to_all.34.blocks = bf16[4,64,1024]{2,1,0:T(8,128)(2,1)S(1)} all-to-all(bf16[4,64,1024]{2,1,0:T(8,128)(2,1)S(1)} %bitcast.13), channel_id=1, replica_groups=mesh['zf'=8,'zn'=2,'yl'=2,'x'=4,'yh'=2,'core'=2] {'zn','yl'}, dimensions={0} | all-to-all | bytes 1048576 | tf_op jit(solution)/shard_map/all_to_all | solution.py:39
  86.4 0.7 shard_map.82.after
  87.2 11.7 %all-to-all-start.5 = ((bf16[8,8,1024]{2,1,0:T(8,128)(2,1)}), bf16[8,8,1024]{2,1,0:T(8,128)(2,1)S(1)}, u32[]{:S(2)}, u32[]{:S(2)}) async-start(bf16[8,8,1024]{2,1,0:T(8,128)(2,1)} %bitcast.3), calls=%async_computation.5 | async-start | bytes 262144 | tf_op jit(solution)/shard_map/all_to_all | solution.py:39
  98.9 0.1 shard_map.83
  99.0 1.4 %convolution_convert_fusion.1 = bf16[512,1024]{1,0:T(8,128)(2,1)} fusion(bf16[256,512]{1,0:T(8,128)(2,1)S(1)} %get-tuple-element.8, bf16[256,1024]{1,0:T(8,128)(2,1)S(1)} %get-tuple-element.9), kind=kOutput, calls=%fused_computation.1 | convolution fusion | flops 268959744 | bytes 1835008 | tf_op jit(solution)/shard_map/dot_general | solution.py:35
  100.4 1.4 %convolution_convert_fusion = bf16[1024,512]{1,0:T(8,128)(2,1)} fusion(bf16[256,1024]{1,0:T(8,128)(2,1)S(1)} %get-tuple-element.10, bf16[256,512]{1,0:T(8,128)(2,1)S(1)} %get-tuple-element.11), kind=kOutput, calls=%fused_computation | convolution fusion | flops 268959744 | bytes 1835008 | tf_op jit(solution)/shard_map/dot_general | solution.py:35
  101.8 4.3 %all-to-all-done.5 = bf16[8,8,1024]{2,1,0:T(8,128)(2,1)S(1)} async-done(((bf16[8,8,1024]{2,1,0:T(8,128)(2,1)}), bf16[8,8,1024]{2,1,0:T(8,128)(2,1)S(1)}, u32[]{:S(2)}, u32[]{:S(2)}) %all-to-all-start.5) | async-done | bytes 131104 | tf_op jit(solution)/shard_map/all_to_all | solution.py:39
  106.1 0.6 fusion.1
  (3 shorter events, 0.1 us)
Async XLA Ops:
  1.3 34.5 %copy-start = (bf16[512,1024]{1,0:T(8,128)(2,1)S(1)}, bf16[512,1024]{1,0:T(8,128)(2,1)}, u32[]{:S(2)}) copy-start(bf16[512,1024]{1,0:T(8,128)(2,1)} %w_up.7) | copy-start | bytes 3145732
  1.4 34.5 %copy-start.1 = (bf16[1024,512]{1,0:T(8,128)(2,1)S(1)}, bf16[1024,512]{1,0:T(8,128)(2,1)}, u32[]{:S(2)}) copy-start(bf16[1024,512]{1,0:T(8,128)(2,1)} %w_down.7) | copy-start | bytes 3145732
  36.5 3.8 %collective-permute-start = (bf16[8,32,1024]{2,1,0:T(8,128)(2,1)S(1)}, bf16[8,32,1024]{2,1,0:T(8,128)(2,1)S(1)}, u32[]{:S(2)}, u32[]{:S(2)}) collective-permute-start(bf16[8,32,1024]{2,1,0:T(8,128)(2,1)S(1)} %shard_map.77), channel_id=1, source_target_pairs={{0,1},{1,0},{2,3},{3,2},{4,5},{5,4},{6,7},{7,6},{8,9},{9,8},{10,11... | collective-permute-start | bytes 1572872 | tf_op jit(solution)/shard_map/ppermute | solution.py:54
  70.5 3.8 %collective-permute-start.1 = (bf16[8,32,1024]{2,1,0:T(8,128)(2,1)S(1)}, bf16[8,32,1024]{2,1,0:T(8,128)(2,1)S(1)}, u32[]{:S(2)}, u32[]{:S(2)}) collective-permute-start(bf16[8,32,1024]{2,1,0:T(8,128)(2,1)S(1)} %all_to_all.33.half), channel_id=1, source_target_pairs={{0,1},{1,0},{2,3},{3,2},{4,5},{5,4},{6,7},{7,6},{8,9},{9,8},{10,11... | collective-permute-start | bytes 1572872 | tf_op jit(solution)/shard_map/ppermute | solution.py:54
  87.2 19.0 %all-to-all-start.5 = ((bf16[8,8,1024]{2,1,0:T(8,128)(2,1)}), bf16[8,8,1024]{2,1,0:T(8,128)(2,1)S(1)}, u32[]{:S(2)}, u32[]{:S(2)}) async-start(bf16[8,8,1024]{2,1,0:T(8,128)(2,1)} %bitcast.3), calls=%async_computation.5 | async-start | bytes 262144 | tf_op jit(solution)/shard_map/all_to_all | solution.py:39

commit v5 on v4

--- a/solution.py
+++ b/solution.py
@@ -12,8 +12,9 @@
 DP = ("x", "yh", "core")
 FAR = "zf"
 NEAR = ("zn", "yl")
-PLANE = ("x", "yh")
-ORDER = (5, 6, 7, 0, 1, 2, 3, 4)
+ORDER = (5, 1, 6, 2, 7, 3, 0, 4)
+PLANES = ("core", "x", "yh")
+GROUPS = ((0, 4, 1, 5, 2, 6, 3, 7), (15, 14, 13, 12, 11, 10, 9, 8))
 F32 = jnp.float32
 BF16 = jnp.bfloat16
 
@@ -82,8 +83,8 @@
 
 def first_half(full, w_up, w_down, out):
     hidden, grad_act = partials(full, w_up, w_down, False)
-    out[:, :16] = hidden.astype(BF16)
-    out[:, 16:] = grad_act.astype(BF16)
+    out[:, :16] = hidden
+    out[:, 16:] = grad_act
 
 
 def second_half(full, w_up, w_down, out):
@@ -91,7 +92,7 @@
 
 
 def add_received(mine, received, out):
-    out[...] = (mine[...] + received[...].astype(F32)).astype(BF16)
+    out[...] = (mine[...] + received[...]).astype(BF16)
 
 
 def activate(blocks, out):
@@ -149,10 +150,10 @@
     pair = jnp.concatenate([inputs, cotangent], axis=1)
     far = spread(pair, FAR, 8, [ORDER]).reshape(64, 1024)
     full = trade(call(repeat_four, (4, 64, 1024), far), NEAR).reshape(256, 1024)
-    received = swap(call(first_half, (8, 32, 1024), full, w_up, w_down))
+    received = swap(call(first_half, (8, 32, 1024), full, w_up, w_down, dtype=F32))
     own = call(second_half, (8, 32, 1024), full, w_up, w_down, dtype=F32)
     summed = call(add_received, (8, 32, 1024), own, received)
-    half = trade(call(activate, (8, 32, 1024), trade(summed, PLANE)), PLANE)
+    half = trade(call(activate, (8, 32, 1024), trade(summed, PLANES, GROUPS)), PLANES, GROUPS)
     half_other = swap(half)
     mine = call(first_out, (128, 1024), half, w_up, w_down)
     parts = call(second_out, (256, 1024), half_other, w_up, w_down, mine).reshape(4, 64, 1024)

time: 109 us -> 107 us (0.982)
  blocking collectives: 75.9 us -> 73.8 us
    all_to_all x5, blocking collectives: 75.9 us -> 73.8 us  [trade(): lax.all_to_all(chunks, axes, 0, 0, axis_index_groups=order, tiled=True)]
where the time goes in v5:
time: 107 us; the launch traced here: 105 us
  blocking collectives  73.8 us (69%)
  starting transfers between devices  15.5 us (14%)
  waiting for transfers between devices  6.77 us (6%)
  Pallas kernels  3.62 us (3%)
  matrix products  2.87 us (3%)
    all_to_all x5, blocking collectives, trade(): lax.all_to_all(chunks, axes, 0, 0, axis_index_groups=order, tiled=True)  73.8 us
    all_to_all x1, starting transfers between devices, trade(): lax.all_to_all(chunks, axes, 0, 0, axis_index_groups=order, tiled=True)  11.6 us
    ppermute x2, starting transfers between devices, swap(): return lax.ppermute(block, 'core', [(0, 1), (1, 0)])  3.83 us
    pallas_call x9, Pallas kernels, call(): pl.pallas_call(body, out_shape=shape, in_specs=[pl.BlockSpec(memory_space...  3.62 us
    all_to_all x1, waiting for transfers between devices, trade(): lax.all_to_all(chunks, axes, 0, 0, axis_index_groups=order, tiled=True)  3.56 us
    ppermute x2, waiting for transfers between devices, swap(): return lax.ppermute(block, 'core', [(0, 1), (1, 0)])  3.21 us
    dot_general x2, matrix products, dot(): lax.dot_general(a, b, (((ca,), (cb,)), ((), ())), preferred_element_type=...  2.87 us
  transfers between devices with their start and end apart: 3, of which 3 were waited for; matrix products, arithmetic and copies ran while one was open for 3% of the time, Pallas kernels for 1%

profile of v5, /device:TPU:6, one launch (start us, length us, event | category | flops | bytes accessed | tf_op | source)
XLA Modules:
  0.0 104.6 jit_solution(13173129994730933635)
XLA Ops:
  0.6 0.7 pad_maximum_fusion
  1.3 0.0 copy-start
  1.4 0.0 copy-start.1
  1.4 23.7 %all_to_all.30 = bf16[8,8,1024]{2,1,0:T(8,128)(2,1)S(1)} all-to-all(bf16[8,8,1024]{2,1,0:T(8,128)(2,1)S(1)} %broadcast_in_dim.2), channel_id=1, replica_groups={{320,64,384,128,448,192,0,256},{321,65,385,129,449,193,1,257},{322,66,3..., dimensions={0} | all-to-all | bytes 262144 | tf_op jit(solution)/shard_map/all_to_all | solution.py:40
  25.1 10.4 %all_to_all.31 = bf16[4,64,1024]{2,1,0:T(8,128)(2,1)S(1)} all-to-all(bf16[4,64,1024]{2,1,0:T(8,128)(2,1)S(1)} %shard_map.75), channel_id=1, replica_groups=mesh['zf'=8,'zn'=2,'yl'=2,'x'=4,'yh'=2,'core'=2] {'zn','yl'}, dimensions={0} | all-to-all | bytes 1048576 | tf_op jit(solution)/shard_map/all_to_all | solution.py:40
  35.6 0.0 copy-done
  35.6 0.0 copy-done.1
  35.6 0.6 shard_map.77
  36.2 1.9 %collective-permute-start = (f32[8,32,1024]{2,1,0:T(8,128)S(1)}, f32[8,32,1024]{2,1,0:T(8,128)S(1)}, u32[]{:S(2)}, u32[]{:S(2)}) collective-permute-start(f32[8,32,1024]{2,1,0:T(8,128)S(1)} %shard_map.77), channel_id=1, source_target_pairs={{0,1},{1,0},{2,3},{3,2},{4,5},{5,4},{6,7},{7,6},{8,9},{9,8},{10,11... | collective-permute-start | bytes 3145736 | tf_op jit(solution)/shard_map/ppermute | solution.py:55
  38.1 0.6 shard_map.76.mine
  38.8 2.0 %collective-permute-done.received = f32[8,32,1024]{2,1,0:T(8,128)S(1)} collective-permute-done((f32[8,32,1024]{2,1,0:T(8,128)S(1)}, f32[8,32,1024]{2,1,0:T(8,128)S(1)}, u32[]{:S(2)}, u32[]{:S(2)}) %collective-permute-start) | collective-permute-done | bytes 1048608 | tf_op jit(solution)/shard_map/ppermute | solution.py:55
  40.8 0.1 shard_map.78
  40.9 14.5 %all_to_all.32.blocks = bf16[8,32,1024]{2,1,0:T(8,128)(2,1)S(1)} all-to-all(bf16[8,32,1024]{2,1,0:T(8,128)(2,1)S(1)} %shard_map.78), channel_id=1, replica_groups={{0,8,2,10,4,12,6,14},{15,13,11,9,7,5,3,1},{16,24,18,26,20,28,22,30},{31..., dimensions={0} | all-to-all | bytes 1048576 | tf_op jit(solution)/shard_map/all_to_all | solution.py:40
  55.3 0.1 shard_map.79
  55.4 13.7 %all_to_all.33.half = bf16[8,32,1024]{2,1,0:T(8,128)(2,1)S(1)} all-to-all(bf16[8,32,1024]{2,1,0:T(8,128)(2,1)S(1)} %shard_map.79), channel_id=1, replica_groups={{0,8,2,10,4,12,6,14},{15,13,11,9,7,5,3,1},{16,24,18,26,20,28,22,30},{31..., dimensions={0} | all-to-all | bytes 1048576 | tf_op jit(solution)/shard_map/all_to_all | solution.py:40
  69.2 1.9 %collective-permute-start.1 = (bf16[8,32,1024]{2,1,0:T(8,128)(2,1)S(1)}, bf16[8,32,1024]{2,1,0:T(8,128)(2,1)S(1)}, u32[]{:S(2)}, u32[]{:S(2)}) collective-permute-start(bf16[8,32,1024]{2,1,0:T(8,128)(2,1)S(1)} %all_to_all.33.half), channel_id=1, source_target_pairs={{0,1},{1,0},{2,3},{3,2},{4,5},{5,4},{6,7},{7,6},{8,9},{9,8},{10,11... | collective-permute-start | bytes 1572872 | tf_op jit(solution)/shard_map/ppermute | solution.py:55
  71.1 0.6 shard_map.80.mine
  71.7 1.2 %collective-permute-done.1.half.half_other = bf16[8,32,1024]{2,1,0:T(8,128)(2,1)S(1)} collective-permute-done((bf16[8,32,1024]{2,1,0:T(8,128)(2,1)S(1)}, bf16[8,32,1024]{2,1,0:T(8,128)(2,1)S(1)}, u32[]{:S(2)}, u32[]{:S(2)}) %collective-permute-start.1) | collective-permute-done | bytes 524320 | tf_op jit(solution)/shard_map/ppermute | solution.py:55
  73.0 0.6 shard_map.81
  73.6 11.5 %all_to_all.34.blocks = bf16[4,64,1024]{2,1,0:T(8,128)(2,1)S(1)} all-to-all(bf16[4,64,1024]{2,1,0:T(8,128)(2,1)S(1)} %bitcast.13), channel_id=1, replica_groups=mesh['zf'=8,'zn'=2,'yl'=2,'x'=4,'yh'=2,'core'=2] {'zn','yl'}, dimensions={0} | all-to-all | bytes 1048576 | tf_op jit(solution)/shard_map/all_to_all | solution.py:40
  85.1 0.7 shard_map.82.after
  85.8 11.6 %all-to-all-start.5 = ((bf16[8,8,1024]{2,1,0:T(8,128)(2,1)}), bf16[8,8,1024]{2,1,0:T(8,128)(2,1)S(1)}, u32[]{:S(2)}, u32[]{:S(2)}) async-start(bf16[8,8,1024]{2,1,0:T(8,128)(2,1)} %bitcast.3), calls=%async_computation.5 | async-start | bytes 262144 | tf_op jit(solution)/shard_map/all_to_all | solution.py:40
  97.5 0.1 shard_map.83
  97.6 1.4 %convolution_convert_fusion = bf16[1024,512]{1,0:T(8,128)(2,1)} fusion(bf16[256,1024]{1,0:T(8,128)(2,1)S(1)} %get-tuple-element.10, bf16[256,512]{1,0:T(8,128)(2,1)S(1)} %get-tuple-element.11), kind=kOutput, calls=%fused_computation | convolution fusion | flops 268959744 | bytes 1835008 | tf_op jit(solution)/shard_map/dot_general | solution.py:36
  99.0 1.4 %convolution_convert_fusion.1 = bf16[512,1024]{1,0:T(8,128)(2,1)} fusion(bf16[256,512]{1,0:T(8,128)(2,1)S(1)} %get-tuple-element.8, bf16[256,1024]{1,0:T(8,128)(2,1)S(1)} %get-tuple-element.9), kind=kOutput, calls=%fused_computation.1 | convolution fusion | flops 268959744 | bytes 1835008 | tf_op jit(solution)/shard_map/dot_general | solution.py:36
  100.4 3.6 %all-to-all-done.5 = bf16[8,8,1024]{2,1,0:T(8,128)(2,1)S(1)} async-done(((bf16[8,8,1024]{2,1,0:T(8,128)(2,1)}), bf16[8,8,1024]{2,1,0:T(8,128)(2,1)S(1)}, u32[]{:S(2)}, u32[]{:S(2)}) %all-to-all-start.5) | async-done | bytes 131104 | tf_op jit(solution)/shard_map/all_to_all | solution.py:40
  104.0 0.6 fusion.1
  (3 shorter events, 0.1 us)
Async XLA Ops:
  1.3 34.2 %copy-start = (bf16[512,1024]{1,0:T(8,128)(2,1)S(1)}, bf16[512,1024]{1,0:T(8,128)(2,1)}, u32[]{:S(2)}) copy-start(bf16[512,1024]{1,0:T(8,128)(2,1)} %w_up.7) | copy-start | bytes 3145732
  1.4 34.2 %copy-start.1 = (bf16[1024,512]{1,0:T(8,128)(2,1)S(1)}, bf16[1024,512]{1,0:T(8,128)(2,1)}, u32[]{:S(2)}) copy-start(bf16[1024,512]{1,0:T(8,128)(2,1)} %w_down.7) | copy-start | bytes 3145732
  36.2 4.6 %collective-permute-start = (f32[8,32,1024]{2,1,0:T(8,128)S(1)}, f32[8,32,1024]{2,1,0:T(8,128)S(1)}, u32[]{:S(2)}, u32[]{:S(2)}) collective-permute-start(f32[8,32,1024]{2,1,0:T(8,128)S(1)} %shard_map.77), channel_id=1, source_target_pairs={{0,1},{1,0},{2,3},{3,2},{4,5},{5,4},{6,7},{7,6},{8,9},{9,8},{10,11... | collective-permute-start | bytes 3145736 | tf_op jit(solution)/shard_map/ppermute | solution.py:55
  69.2 3.8 %collective-permute-start.1 = (bf16[8,32,1024]{2,1,0:T(8,128)(2,1)S(1)}, bf16[8,32,1024]{2,1,0:T(8,128)(2,1)S(1)}, u32[]{:S(2)}, u32[]{:S(2)}) collective-permute-start(bf16[8,32,1024]{2,1,0:T(8,128)(2,1)S(1)} %all_to_all.33.half), channel_id=1, source_target_pairs={{0,1},{1,0},{2,3},{3,2},{4,5},{5,4},{6,7},{7,6},{8,9},{9,8},{10,11... | collective-permute-start | bytes 1572872 | tf_op jit(solution)/shard_map/ppermute | solution.py:55
  85.8 18.2 %all-to-all-start.5 = ((bf16[8,8,1024]{2,1,0:T(8,128)(2,1)}), bf16[8,8,1024]{2,1,0:T(8,128)(2,1)S(1)}, u32[]{:S(2)}, u32[]{:S(2)}) async-start(bf16[8,8,1024]{2,1,0:T(8,128)(2,1)} %bitcast.3), calls=%async_computation.5 | async-start | bytes 262144 | tf_op jit(solution)/shard_map/all_to_all | solution.py:40

commit v6 on v5

--- a/solution.py
+++ b/solution.py
@@ -13,8 +13,8 @@
 FAR = "zf"
 NEAR = ("zn", "yl")
 ORDER = (5, 1, 6, 2, 7, 3, 0, 4)
-PLANES = ("core", "x", "yh")
-GROUPS = ((0, 4, 1, 5, 2, 6, 3, 7), (15, 14, 13, 12, 11, 10, 9, 8))
+PLANE = ("x", "yh")
+PLANE_ORDER = (7, 3, 6, 2, 5, 1, 4, 0)
 F32 = jnp.float32
 BF16 = jnp.bfloat16
 
@@ -153,7 +153,7 @@
     received = swap(call(first_half, (8, 32, 1024), full, w_up, w_down, dtype=F32))
     own = call(second_half, (8, 32, 1024), full, w_up, w_down, dtype=F32)
     summed = call(add_received, (8, 32, 1024), own, received)
-    half = trade(call(activate, (8, 32, 1024), trade(summed, PLANES, GROUPS)), PLANES, GROUPS)
+    half = trade(call(activate, (8, 32, 1024), trade(summed, PLANE, [PLANE_ORDER])), PLANE, [PLANE_ORDER])
     half_other = swap(half)
     mine = call(first_out, (128, 1024), half, w_up, w_down)
     parts = call(second_out, (256, 1024), half_other, w_up, w_down, mine).reshape(4, 64, 1024)

time: 107 us -> 105 us (0.981); the launches traced: 105 us -> 104 us
  no operation moved by 1% of the time
where the time goes in v6:
time: 105 us; the launch traced here: 104 us
  blocking collectives  73.6 us (70%)
  starting transfers between devices  15.5 us (15%)
  waiting for transfers between devices  6.77 us (6%)
  Pallas kernels  3.61 us (3%)
  matrix products  2.87 us (3%)
    all_to_all x5, blocking collectives, trade(): lax.all_to_all(chunks, axes, 0, 0, axis_index_groups=order, tiled=True)  73.6 us
    all_to_all x1, starting transfers between devices, trade(): lax.all_to_all(chunks, axes, 0, 0, axis_index_groups=order, tiled=True)  11.6 us
    ppermute x2, starting transfers between devices, swap(): return lax.ppermute(block, 'core', [(0, 1), (1, 0)])  3.83 us
    pallas_call x9, Pallas kernels, call(): pl.pallas_call(body, out_shape=shape, in_specs=[pl.BlockSpec(memory_space...  3.61 us
    all_to_all x1, waiting for transfers between devices, trade(): lax.all_to_all(chunks, axes, 0, 0, axis_index_groups=order, tiled=True)  3.56 us
    ppermute x2, waiting for transfers between devices, swap(): return lax.ppermute(block, 'core', [(0, 1), (1, 0)])  3.21 us
    dot_general x2, matrix products, dot(): lax.dot_general(a, b, (((ca,), (cb,)), ((), ())), preferred_element_type=...  2.87 us
  transfers between devices with their start and end apart: 3, of which 3 were waited for; matrix products, arithmetic and copies ran while one was open for 3% of the time, Pallas kernels for 1%

profile of v6, /device:TPU:6, one launch (start us, length us, event | category | flops | bytes accessed | tf_op | source)
XLA Modules:
  0.0 104.4 jit_solution(5507488895924578570)
XLA Ops:
  0.6 0.7 pad_maximum_fusion
  1.3 0.0 copy-start
  1.4 0.0 copy-start.1
  1.4 23.7 %all_to_all.30 = bf16[8,8,1024]{2,1,0:T(8,128)(2,1)S(1)} all-to-all(bf16[8,8,1024]{2,1,0:T(8,128)(2,1)S(1)} %broadcast_in_dim.2), channel_id=1, replica_groups={{320,64,384,128,448,192,0,256},{321,65,385,129,449,193,1,257},{322,66,3..., dimensions={0} | all-to-all | bytes 262144 | tf_op jit(solution)/shard_map/all_to_all | solution.py:40
  25.1 10.4 %all_to_all.31 = bf16[4,64,1024]{2,1,0:T(8,128)(2,1)S(1)} all-to-all(bf16[4,64,1024]{2,1,0:T(8,128)(2,1)S(1)} %shard_map.75), channel_id=1, replica_groups=mesh['zf'=8,'zn'=2,'yl'=2,'x'=4,'yh'=2,'core'=2] {'zn','yl'}, dimensions={0} | all-to-all | bytes 1048576 | tf_op jit(solution)/shard_map/all_to_all | solution.py:40
  35.6 0.0 copy-done
  35.6 0.0 copy-done.1
  35.6 0.6 shard_map.77
  36.2 1.9 %collective-permute-start = (f32[8,32,1024]{2,1,0:T(8,128)S(1)}, f32[8,32,1024]{2,1,0:T(8,128)S(1)}, u32[]{:S(2)}, u32[]{:S(2)}) collective-permute-start(f32[8,32,1024]{2,1,0:T(8,128)S(1)} %shard_map.77), channel_id=1, source_target_pairs={{0,1},{1,0},{2,3},{3,2},{4,5},{5,4},{6,7},{7,6},{8,9},{9,8},{10,11... | collective-permute-start | bytes 3145736 | tf_op jit(solution)/shard_map/ppermute | solution.py:55
  38.1 0.6 shard_map.76.mine
  38.8 2.0 %collective-permute-done.received = f32[8,32,1024]{2,1,0:T(8,128)S(1)} collective-permute-done((f32[8,32,1024]{2,1,0:T(8,128)S(1)}, f32[8,32,1024]{2,1,0:T(8,128)S(1)}, u32[]{:S(2)}, u32[]{:S(2)}) %collective-permute-start) | collective-permute-done | bytes 1048608 | tf_op jit(solution)/shard_map/ppermute | solution.py:55
  40.8 0.1 shard_map.78
  40.9 14.5 %all_to_all.32.blocks = bf16[8,32,1024]{2,1,0:T(8,128)(2,1)S(1)} all-to-all(bf16[8,32,1024]{2,1,0:T(8,128)(2,1)S(1)} %shard_map.78), channel_id=1, replica_groups={{14,6,12,4,10,2,8,0},{15,7,13,5,11,3,9,1},{30,22,28,20,26,18,24,16},{31..., dimensions={0} | all-to-all | bytes 1048576 | tf_op jit(solution)/shard_map/all_to_all | solution.py:40
  55.4 0.1 shard_map.79
  55.5 13.4 %all_to_all.33.half = bf16[8,32,1024]{2,1,0:T(8,128)(2,1)S(1)} all-to-all(bf16[8,32,1024]{2,1,0:T(8,128)(2,1)S(1)} %shard_map.79), channel_id=1, replica_groups={{14,6,12,4,10,2,8,0},{15,7,13,5,11,3,9,1},{30,22,28,20,26,18,24,16},{31..., dimensions={0} | all-to-all | bytes 1048576 | tf_op jit(solution)/shard_map/all_to_all | solution.py:40
  69.0 1.9 %collective-permute-start.1 = (bf16[8,32,1024]{2,1,0:T(8,128)(2,1)S(1)}, bf16[8,32,1024]{2,1,0:T(8,128)(2,1)S(1)}, u32[]{:S(2)}, u32[]{:S(2)}) collective-permute-start(bf16[8,32,1024]{2,1,0:T(8,128)(2,1)S(1)} %all_to_all.33.half), channel_id=1, source_target_pairs={{0,1},{1,0},{2,3},{3,2},{4,5},{5,4},{6,7},{7,6},{8,9},{9,8},{10,11... | collective-permute-start | bytes 1572872 | tf_op jit(solution)/shard_map/ppermute | solution.py:55
  70.9 0.6 shard_map.80.mine
  71.5 1.2 %collective-permute-done.1.half.half_other = bf16[8,32,1024]{2,1,0:T(8,128)(2,1)S(1)} collective-permute-done((bf16[8,32,1024]{2,1,0:T(8,128)(2,1)S(1)}, bf16[8,32,1024]{2,1,0:T(8,128)(2,1)S(1)}, u32[]{:S(2)}, u32[]{:S(2)}) %collective-permute-start.1) | collective-permute-done | bytes 524320 | tf_op jit(solution)/shard_map/ppermute | solution.py:55
  72.7 0.6 shard_map.81
  73.4 11.5 %all_to_all.34.blocks = bf16[4,64,1024]{2,1,0:T(8,128)(2,1)S(1)} all-to-all(bf16[4,64,1024]{2,1,0:T(8,128)(2,1)S(1)} %bitcast.13), channel_id=1, replica_groups=mesh['zf'=8,'zn'=2,'yl'=2,'x'=4,'yh'=2,'core'=2] {'zn','yl'}, dimensions={0} | all-to-all | bytes 1048576 | tf_op jit(solution)/shard_map/all_to_all | solution.py:40
  84.9 0.7 shard_map.82.after
  85.6 11.6 %all-to-all-start.5 = ((bf16[8,8,1024]{2,1,0:T(8,128)(2,1)}), bf16[8,8,1024]{2,1,0:T(8,128)(2,1)S(1)}, u32[]{:S(2)}, u32[]{:S(2)}) async-start(bf16[8,8,1024]{2,1,0:T(8,128)(2,1)} %bitcast.3), calls=%async_computation.5 | async-start | bytes 262144 | tf_op jit(solution)/shard_map/all_to_all | solution.py:40
  97.2 0.1 shard_map.83
  97.4 1.4 %convolution_convert_fusion = bf16[1024,512]{1,0:T(8,128)(2,1)} fusion(bf16[256,1024]{1,0:T(8,128)(2,1)S(1)} %get-tuple-element.10, bf16[256,512]{1,0:T(8,128)(2,1)S(1)} %get-tuple-element.11), kind=kOutput, calls=%fused_computation | convolution fusion | flops 268959744 | bytes 1835008 | tf_op jit(solution)/shard_map/dot_general | solution.py:36
  98.8 1.4 %convolution_convert_fusion.1 = bf16[512,1024]{1,0:T(8,128)(2,1)} fusion(bf16[256,512]{1,0:T(8,128)(2,1)S(1)} %get-tuple-element.8, bf16[256,1024]{1,0:T(8,128)(2,1)S(1)} %get-tuple-element.9), kind=kOutput, calls=%fused_computation.1 | convolution fusion | flops 268959744 | bytes 1835008 | tf_op jit(solution)/shard_map/dot_general | solution.py:36
  100.2 3.6 %all-to-all-done.5 = bf16[8,8,1024]{2,1,0:T(8,128)(2,1)S(1)} async-done(((bf16[8,8,1024]{2,1,0:T(8,128)(2,1)}), bf16[8,8,1024]{2,1,0:T(8,128)(2,1)S(1)}, u32[]{:S(2)}, u32[]{:S(2)}) %all-to-all-start.5) | async-done | bytes 131104 | tf_op jit(solution)/shard_map/all_to_all | solution.py:40
  103.8 0.6 fusion.1
  (3 shorter events, 0.1 us)
Async XLA Ops:
  1.3 34.2 %copy-start = (bf16[512,1024]{1,0:T(8,128)(2,1)S(1)}, bf16[512,1024]{1,0:T(8,128)(2,1)}, u32[]{:S(2)}) copy-start(bf16[512,1024]{1,0:T(8,128)(2,1)} %w_up.7) | copy-start | bytes 3145732
  1.4 34.2 %copy-start.1 = (bf16[1024,512]{1,0:T(8,128)(2,1)S(1)}, bf16[1024,512]{1,0:T(8,128)(2,1)}, u32[]{:S(2)}) copy-start(bf16[1024,512]{1,0:T(8,128)(2,1)} %w_down.7) | copy-start | bytes 3145732
  36.2 4.6 %collective-permute-start = (f32[8,32,1024]{2,1,0:T(8,128)S(1)}, f32[8,32,1024]{2,1,0:T(8,128)S(1)}, u32[]{:S(2)}, u32[]{:S(2)}) collective-permute-start(f32[8,32,1024]{2,1,0:T(8,128)S(1)} %shard_map.77), channel_id=1, source_target_pairs={{0,1},{1,0},{2,3},{3,2},{4,5},{5,4},{6,7},{7,6},{8,9},{9,8},{10,11... | collective-permute-start | bytes 3145736 | tf_op jit(solution)/shard_map/ppermute | solution.py:55
  69.0 3.8 %collective-permute-start.1 = (bf16[8,32,1024]{2,1,0:T(8,128)(2,1)S(1)}, bf16[8,32,1024]{2,1,0:T(8,128)(2,1)S(1)}, u32[]{:S(2)}, u32[]{:S(2)}) collective-permute-start(bf16[8,32,1024]{2,1,0:T(8,128)(2,1)S(1)} %all_to_all.33.half), channel_id=1, source_target_pairs={{0,1},{1,0},{2,3},{3,2},{4,5},{5,4},{6,7},{7,6},{8,9},{9,8},{10,11... | collective-permute-start | bytes 1572872 | tf_op jit(solution)/shard_map/ppermute | solution.py:55
  85.6 18.2 %all-to-all-start.5 = ((bf16[8,8,1024]{2,1,0:T(8,128)(2,1)}), bf16[8,8,1024]{2,1,0:T(8,128)(2,1)S(1)}, u32[]{:S(2)}, u32[]{:S(2)}) async-start(bf16[8,8,1024]{2,1,0:T(8,128)(2,1)} %bitcast.3), calls=%async_computation.5 | async-start | bytes 262144 | tf_op jit(solution)/shard_map/all_to_all | solution.py:40

commit v7 on v6

--- a/solution.py
+++ b/solution.py
@@ -83,8 +83,10 @@
 
 def first_half(full, w_up, w_down, out):
     hidden, grad_act = partials(full, w_up, w_down, False)
-    out[:, :16] = hidden
-    out[:, 16:] = grad_act
+    out[:, :16] = hidden.astype(BF16)
+    high = grad_act.astype(BF16)
+    out[:, 16:32] = high
+    out[:, 32:] = (grad_act - high.astype(F32)).astype(BF16)
 
 
 def second_half(full, w_up, w_down, out):
@@ -92,7 +94,9 @@
 
 
 def add_received(mine, received, out):
-    out[...] = (mine[...] + received[...]).astype(BF16)
+    got = received[...].astype(F32)
+    out[:, :16] = (mine[:, :16] + got[:, :16]).astype(BF16)
+    out[:, 16:] = (mine[:, 16:] + (got[:, 16:32] + got[:, 32:])).astype(BF16)
 
 
 def activate(blocks, out):
@@ -150,7 +154,7 @@
     pair = jnp.concatenate([inputs, cotangent], axis=1)
     far = spread(pair, FAR, 8, [ORDER]).reshape(64, 1024)
     full = trade(call(repeat_four, (4, 64, 1024), far), NEAR).reshape(256, 1024)
-    received = swap(call(first_half, (8, 32, 1024), full, w_up, w_down, dtype=F32))
+    received = swap(call(first_half, (8, 48, 1024), full, w_up, w_down))
     own = call(second_half, (8, 32, 1024), full, w_up, w_down, dtype=F32)
     summed = call(add_received, (8, 32, 1024), own, received)
     half = trade(call(activate, (8, 32, 1024), trade(summed, PLANE, [PLANE_ORDER])), PLANE, [PLANE_ORDER])

time: 105 us -> 105 us (level)
  no operation moved by 1% of the time
where the time goes in v7:
time: 105 us; the launch traced here: 104 us
  blocking collectives  73.6 us (70%)
  starting transfers between devices  15.5 us (15%)
  waiting for transfers between devices  6.4 us (6%)
  Pallas kernels  3.65 us (3%)
  matrix products  2.87 us (3%)
    all_to_all x5, blocking collectives, trade(): lax.all_to_all(chunks, axes, 0, 0, axis_index_groups=order, tiled=True)  73.6 us
    all_to_all x1, starting transfers between devices, trade(): lax.all_to_all(chunks, axes, 0, 0, axis_index_groups=order, tiled=True)  11.6 us
    ppermute x2, starting transfers between devices, swap(): return lax.ppermute(block, 'core', [(0, 1), (1, 0)])  3.83 us
    pallas_call x9, Pallas kernels, call(): pl.pallas_call(body, out_shape=shape, in_specs=[pl.BlockSpec(memory_space...  3.65 us
    all_to_all x1, waiting for transfers between devices, trade(): lax.all_to_all(chunks, axes, 0, 0, axis_index_groups=order, tiled=True)  3.56 us
    dot_general x2, matrix products, dot(): lax.dot_general(a, b, (((ca,), (cb,)), ((), ())), preferred_element_type=...  2.87 us
    ppermute x2, waiting for transfers between devices, swap(): return lax.ppermute(block, 'core', [(0, 1), (1, 0)])  2.84 us
  transfers between devices with their start and end apart: 3, of which 3 were waited for; matrix products, arithmetic and copies ran while one was open for 3% of the time, Pallas kernels for 1%

profile of v7, /device:TPU:6, one launch (start us, length us, event | category | flops | bytes accessed | tf_op | source)
XLA Modules:
  0.0 104.1 jit_solution(11126828082118865994)
XLA Ops:
  0.6 0.7 pad_maximum_fusion
  1.3 0.0 copy-start
  1.4 0.0 copy-start.1
  1.4 23.7 %all_to_all.30 = bf16[8,8,1024]{2,1,0:T(8,128)(2,1)S(1)} all-to-all(bf16[8,8,1024]{2,1,0:T(8,128)(2,1)S(1)} %broadcast_in_dim.2), channel_id=1, replica_groups={{320,64,384,128,448,192,0,256},{321,65,385,129,449,193,1,257},{322,66,3..., dimensions={0} | all-to-all | bytes 262144 | tf_op jit(solution)/shard_map/all_to_all | solution.py:40
  25.1 10.4 %all_to_all.31 = bf16[4,64,1024]{2,1,0:T(8,128)(2,1)S(1)} all-to-all(bf16[4,64,1024]{2,1,0:T(8,128)(2,1)S(1)} %shard_map.75), channel_id=1, replica_groups=mesh['zf'=8,'zn'=2,'yl'=2,'x'=4,'yh'=2,'core'=2] {'zn','yl'}, dimensions={0} | all-to-all | bytes 1048576 | tf_op jit(solution)/shard_map/all_to_all | solution.py:40
  35.6 0.0 copy-done
  35.6 0.0 copy-done.1
  35.6 0.6 shard_map.77
  36.2 1.9 %collective-permute-start = (bf16[8,48,1024]{2,1,0:T(8,128)(2,1)S(1)}, bf16[8,48,1024]{2,1,0:T(8,128)(2,1)S(1)}, u32[]{:S(2)}, u32[]{:S(2)}) collective-permute-start(bf16[8,48,1024]{2,1,0:T(8,128)(2,1)S(1)} %shard_map.77), channel_id=1, source_target_pairs={{0,1},{1,0},{2,3},{3,2},{4,5},{5,4},{6,7},{7,6},{8,9},{9,8},{10,11... | collective-permute-start | bytes 2359304 | tf_op jit(solution)/shard_map/ppermute | solution.py:55
  38.2 0.6 shard_map.76.mine
  38.8 1.6 %collective-permute-done.received = bf16[8,48,1024]{2,1,0:T(8,128)(2,1)S(1)} collective-permute-done((bf16[8,48,1024]{2,1,0:T(8,128)(2,1)S(1)}, bf16[8,48,1024]{2,1,0:T(8,128)(2,1)S(1)}, u32[]{:S(2)}, u32[]{:S(2)}) %collective-permute-start) | collective-permute-done | bytes 786464 | tf_op jit(solution)/shard_map/ppermute | solution.py:55
  40.4 0.1 shard_map.78
  40.5 14.5 %all_to_all.32.blocks = bf16[8,32,1024]{2,1,0:T(8,128)(2,1)S(1)} all-to-all(bf16[8,32,1024]{2,1,0:T(8,128)(2,1)S(1)} %shard_map.78), channel_id=1, replica_groups={{14,6,12,4,10,2,8,0},{15,7,13,5,11,3,9,1},{30,22,28,20,26,18,24,16},{31..., dimensions={0} | all-to-all | bytes 1048576 | tf_op jit(solution)/shard_map/all_to_all | solution.py:40
  55.0 0.1 shard_map.79
  55.2 13.4 %all_to_all.33.half = bf16[8,32,1024]{2,1,0:T(8,128)(2,1)S(1)} all-to-all(bf16[8,32,1024]{2,1,0:T(8,128)(2,1)S(1)} %shard_map.79), channel_id=1, replica_groups={{14,6,12,4,10,2,8,0},{15,7,13,5,11,3,9,1},{30,22,28,20,26,18,24,16},{31..., dimensions={0} | all-to-all | bytes 1048576 | tf_op jit(solution)/shard_map/all_to_all | solution.py:40
  68.6 1.9 %collective-permute-start.1 = (bf16[8,32,1024]{2,1,0:T(8,128)(2,1)S(1)}, bf16[8,32,1024]{2,1,0:T(8,128)(2,1)S(1)}, u32[]{:S(2)}, u32[]{:S(2)}) collective-permute-start(bf16[8,32,1024]{2,1,0:T(8,128)(2,1)S(1)} %all_to_all.33.half), channel_id=1, source_target_pairs={{0,1},{1,0},{2,3},{3,2},{4,5},{5,4},{6,7},{7,6},{8,9},{9,8},{10,11... | collective-permute-start | bytes 1572872 | tf_op jit(solution)/shard_map/ppermute | solution.py:55
  70.5 0.6 shard_map.80.mine
  71.2 1.2 %collective-permute-done.1.half.half_other = bf16[8,32,1024]{2,1,0:T(8,128)(2,1)S(1)} collective-permute-done((bf16[8,32,1024]{2,1,0:T(8,128)(2,1)S(1)}, bf16[8,32,1024]{2,1,0:T(8,128)(2,1)S(1)}, u32[]{:S(2)}, u32[]{:S(2)}) %collective-permute-start.1) | collective-permute-done | bytes 524320 | tf_op jit(solution)/shard_map/ppermute | solution.py:55
  72.4 0.6 shard_map.81
  73.1 11.5 %all_to_all.34.blocks = bf16[4,64,1024]{2,1,0:T(8,128)(2,1)S(1)} all-to-all(bf16[4,64,1024]{2,1,0:T(8,128)(2,1)S(1)} %bitcast.13), channel_id=1, replica_groups=mesh['zf'=8,'zn'=2,'yl'=2,'x'=4,'yh'=2,'core'=2] {'zn','yl'}, dimensions={0} | all-to-all | bytes 1048576 | tf_op jit(solution)/shard_map/all_to_all | solution.py:40
  84.6 0.7 shard_map.82.after
  85.3 11.6 %all-to-all-start.5 = ((bf16[8,8,1024]{2,1,0:T(8,128)(2,1)}), bf16[8,8,1024]{2,1,0:T(8,128)(2,1)S(1)}, u32[]{:S(2)}, u32[]{:S(2)}) async-start(bf16[8,8,1024]{2,1,0:T(8,128)(2,1)} %bitcast.3), calls=%async_computation.5 | async-start | bytes 262144 | tf_op jit(solution)/shard_map/all_to_all | solution.py:40
  96.9 0.1 shard_map.83
  97.0 1.4 %convolution_convert_fusion.1 = bf16[512,1024]{1,0:T(8,128)(2,1)} fusion(bf16[256,512]{1,0:T(8,128)(2,1)S(1)} %get-tuple-element.8, bf16[256,1024]{1,0:T(8,128)(2,1)S(1)} %get-tuple-element.9), kind=kOutput, calls=%fused_computation.1 | convolution fusion | flops 268959744 | bytes 1835008 | tf_op jit(solution)/shard_map/dot_general | solution.py:36
  98.4 1.4 %convolution_convert_fusion = bf16[1024,512]{1,0:T(8,128)(2,1)} fusion(bf16[256,1024]{1,0:T(8,128)(2,1)S(1)} %get-tuple-element.10, bf16[256,512]{1,0:T(8,128)(2,1)S(1)} %get-tuple-element.11), kind=kOutput, calls=%fused_computation | convolution fusion | flops 268959744 | bytes 1835008 | tf_op jit(solution)/shard_map/dot_general | solution.py:36
  99.9 3.6 %all-to-all-done.5 = bf16[8,8,1024]{2,1,0:T(8,128)(2,1)S(1)} async-done(((bf16[8,8,1024]{2,1,0:T(8,128)(2,1)}), bf16[8,8,1024]{2,1,0:T(8,128)(2,1)S(1)}, u32[]{:S(2)}, u32[]{:S(2)}) %all-to-all-start.5) | async-done | bytes 131104 | tf_op jit(solution)/shard_map/all_to_all | solution.py:40
  103.5 0.6 fusion.1
  (3 shorter events, 0.1 us)
Async XLA Ops:
  1.3 34.2 %copy-start = (bf16[512,1024]{1,0:T(8,128)(2,1)S(1)}, bf16[512,1024]{1,0:T(8,128)(2,1)}, u32[]{:S(2)}) copy-start(bf16[512,1024]{1,0:T(8,128)(2,1)} %w_up.7) | copy-start | bytes 3145732
  1.4 34.2 %copy-start.1 = (bf16[1024,512]{1,0:T(8,128)(2,1)S(1)}, bf16[1024,512]{1,0:T(8,128)(2,1)}, u32[]{:S(2)}) copy-start(bf16[1024,512]{1,0:T(8,128)(2,1)} %w_down.7) | copy-start | bytes 3145732
  36.2 4.2 %collective-permute-start = (bf16[8,48,1024]{2,1,0:T(8,128)(2,1)S(1)}, bf16[8,48,1024]{2,1,0:T(8,128)(2,1)S(1)}, u32[]{:S(2)}, u32[]{:S(2)}) collective-permute-start(bf16[8,48,1024]{2,1,0:T(8,128)(2,1)S(1)} %shard_map.77), channel_id=1, source_target_pairs={{0,1},{1,0},{2,3},{3,2},{4,5},{5,4},{6,7},{7,6},{8,9},{9,8},{10,11... | collective-permute-start | bytes 2359304 | tf_op jit(solution)/shard_map/ppermute | solution.py:55
  68.6 3.8 %collective-permute-start.1 = (bf16[8,32,1024]{2,1,0:T(8,128)(2,1)S(1)}, bf16[8,32,1024]{2,1,0:T(8,128)(2,1)S(1)}, u32[]{:S(2)}, u32[]{:S(2)}) collective-permute-start(bf16[8,32,1024]{2,1,0:T(8,128)(2,1)S(1)} %all_to_all.33.half), channel_id=1, source_target_pairs={{0,1},{1,0},{2,3},{3,2},{4,5},{5,4},{6,7},{7,6},{8,9},{9,8},{10,11... | collective-permute-start | bytes 1572872 | tf_op jit(solution)/shard_map/ppermute | solution.py:55
  85.3 18.2 %all-to-all-start.5 = ((bf16[8,8,1024]{2,1,0:T(8,128)(2,1)}), bf16[8,8,1024]{2,1,0:T(8,128)(2,1)S(1)}, u32[]{:S(2)}, u32[]{:S(2)}) async-start(bf16[8,8,1024]{2,1,0:T(8,128)(2,1)} %bitcast.3), calls=%async_computation.5 | async-start | bytes 262144 | tf_op jit(solution)/shard_map/all_to_all | solution.py:40

commit v8 on v6

--- a/solution.py
+++ b/solution.py
@@ -12,6 +12,7 @@
 DP = ("x", "yh", "core")
 FAR = "zf"
 NEAR = ("zn", "yl")
+NEAR_ORDER = (3, 2, 1, 0)
 ORDER = (5, 1, 6, 2, 7, 3, 0, 4)
 PLANE = ("x", "yh")
 PLANE_ORDER = (7, 3, 6, 2, 5, 1, 4, 0)
@@ -149,7 +150,7 @@
 def local(inputs, w_up, w_down, cotangent):
     pair = jnp.concatenate([inputs, cotangent], axis=1)
     far = spread(pair, FAR, 8, [ORDER]).reshape(64, 1024)
-    full = trade(call(repeat_four, (4, 64, 1024), far), NEAR).reshape(256, 1024)
+    full = trade(call(repeat_four, (4, 64, 1024), far), NEAR, [NEAR_ORDER]).reshape(256, 1024)
     received = swap(call(first_half, (8, 32, 1024), full, w_up, w_down, dtype=F32))
     own = call(second_half, (8, 32, 1024), full, w_up, w_down, dtype=F32)
     summed = call(add_received, (8, 32, 1024), own, received)
@@ -157,7 +158,7 @@
     half_other = swap(half)
     mine = call(first_out, (128, 1024), half, w_up, w_down)
     parts = call(second_out, (256, 1024), half_other, w_up, w_down, mine).reshape(4, 64, 1024)
-    near = call(add_four, (64, 1024), trade(parts, NEAR))
+    near = call(add_four, (64, 1024), trade(parts, NEAR, [NEAR_ORDER]))
     sums = total(trade(near.reshape(8, 8, 1024), FAR, [ORDER])).astype(BF16)
 
     sizes = [(256, 1024), (256, 1024), (256, 512), (256, 512)]

time: 105 us -> 105 us (level)
  no operation moved by 1% of the time
where the time goes in v8:
time: 105 us; the launch traced here: 104 us
  blocking collectives  72.6 us (69%)
  starting transfers between devices  15.7 us (15%)
  waiting for transfers between devices  7.23 us (7%)
  Pallas kernels  3.61 us (3%)
  matrix products  2.87 us (3%)
    all_to_all x5, blocking collectives, trade(): lax.all_to_all(chunks, axes, 0, 0, axis_index_groups=order, tiled=True)  72.6 us
    all_to_all x1, starting transfers between devices, trade(): lax.all_to_all(chunks, axes, 0, 0, axis_index_groups=order, tiled=True)  11.9 us
    all_to_all x1, waiting for transfers between devices, trade(): lax.all_to_all(chunks, axes, 0, 0, axis_index_groups=order, tiled=True)  4.02 us
    ppermute x2, starting transfers between devices, swap(): return lax.ppermute(block, 'core', [(0, 1), (1, 0)])  3.83 us
    pallas_call x9, Pallas kernels, call(): pl.pallas_call(body, out_shape=shape, in_specs=[pl.BlockSpec(memory_space...  3.61 us
    ppermute x2, waiting for transfers between devices, swap(): return lax.ppermute(block, 'core', [(0, 1), (1, 0)])  3.21 us
    dot_general x2, matrix products, dot(): lax.dot_general(a, b, (((ca,), (cb,)), ((), ())), preferred_element_type=...  2.87 us
  transfers between devices with their start and end apart: 3, of which 3 were waited for; matrix products, arithmetic and copies ran while one was open for 3% of the time, Pallas kernels for 1%

profile of v8, /device:TPU:6, one launch (start us, length us, event | category | flops | bytes accessed | tf_op | source)
XLA Modules:
  0.0 104.2 jit_solution(10973921280320924705)
XLA Ops:
  0.6 0.7 pad_maximum_fusion
  1.3 0.0 copy-start
  1.4 0.0 copy-start.1
  1.4 23.7 %all_to_all.30 = bf16[8,8,1024]{2,1,0:T(8,128)(2,1)S(1)} all-to-all(bf16[8,8,1024]{2,1,0:T(8,128)(2,1)S(1)} %broadcast_in_dim.2), channel_id=1, replica_groups={{320,64,384,128,448,192,0,256},{321,65,385,129,449,193,1,257},{322,66,3..., dimensions={0} | all-to-all | bytes 262144 | tf_op jit(solution)/shard_map/all_to_all | solution.py:41
  25.1 9.7 %all_to_all.31 = bf16[4,64,1024]{2,1,0:T(8,128)(2,1)S(1)} all-to-all(bf16[4,64,1024]{2,1,0:T(8,128)(2,1)S(1)} %shard_map.75), channel_id=1, replica_groups={{48,32,16,0},{49,33,17,1},{50,34,18,2},{51,35,19,3},{52,36,20,4},{53,37..., dimensions={0} | all-to-all | bytes 1048576 | tf_op jit(solution)/shard_map/all_to_all | solution.py:41
  34.9 0.0 copy-done
  34.9 0.0 copy-done.1
  34.9 0.6 shard_map.77
  35.5 1.9 %collective-permute-start = (f32[8,32,1024]{2,1,0:T(8,128)S(1)}, f32[8,32,1024]{2,1,0:T(8,128)S(1)}, u32[]{:S(2)}, u32[]{:S(2)}) collective-permute-start(f32[8,32,1024]{2,1,0:T(8,128)S(1)} %shard_map.77), channel_id=1, source_target_pairs={{0,1},{1,0},{2,3},{3,2},{4,5},{5,4},{6,7},{7,6},{8,9},{9,8},{10,11... | collective-permute-start | bytes 3145736 | tf_op jit(solution)/shard_map/ppermute | solution.py:56
  37.5 0.6 shard_map.76.mine
  38.1 2.0 %collective-permute-done.received = f32[8,32,1024]{2,1,0:T(8,128)S(1)} collective-permute-done((f32[8,32,1024]{2,1,0:T(8,128)S(1)}, f32[8,32,1024]{2,1,0:T(8,128)S(1)}, u32[]{:S(2)}, u32[]{:S(2)}) %collective-permute-start) | collective-permute-done | bytes 1048608 | tf_op jit(solution)/shard_map/ppermute | solution.py:56
  40.1 0.1 shard_map.78
  40.2 14.5 %all_to_all.32.blocks = bf16[8,32,1024]{2,1,0:T(8,128)(2,1)S(1)} all-to-all(bf16[8,32,1024]{2,1,0:T(8,128)(2,1)S(1)} %shard_map.78), channel_id=1, replica_groups={{14,6,12,4,10,2,8,0},{15,7,13,5,11,3,9,1},{30,22,28,20,26,18,24,16},{31..., dimensions={0} | all-to-all | bytes 1048576 | tf_op jit(solution)/shard_map/all_to_all | solution.py:41
  54.7 0.1 shard_map.79
  54.8 13.4 %all_to_all.33.half = bf16[8,32,1024]{2,1,0:T(8,128)(2,1)S(1)} all-to-all(bf16[8,32,1024]{2,1,0:T(8,128)(2,1)S(1)} %shard_map.79), channel_id=1, replica_groups={{14,6,12,4,10,2,8,0},{15,7,13,5,11,3,9,1},{30,22,28,20,26,18,24,16},{31..., dimensions={0} | all-to-all | bytes 1048576 | tf_op jit(solution)/shard_map/all_to_all | solution.py:41
  68.3 1.9 %collective-permute-start.1 = (bf16[8,32,1024]{2,1,0:T(8,128)(2,1)S(1)}, bf16[8,32,1024]{2,1,0:T(8,128)(2,1)S(1)}, u32[]{:S(2)}, u32[]{:S(2)}) collective-permute-start(bf16[8,32,1024]{2,1,0:T(8,128)(2,1)S(1)} %all_to_all.33.half), channel_id=1, source_target_pairs={{0,1},{1,0},{2,3},{3,2},{4,5},{5,4},{6,7},{7,6},{8,9},{9,8},{10,11... | collective-permute-start | bytes 1572872 | tf_op jit(solution)/shard_map/ppermute | solution.py:56
  70.2 0.6 shard_map.80.mine
  70.8 1.2 %collective-permute-done.1.half.half_other = bf16[8,32,1024]{2,1,0:T(8,128)(2,1)S(1)} collective-permute-done((bf16[8,32,1024]{2,1,0:T(8,128)(2,1)S(1)}, bf16[8,32,1024]{2,1,0:T(8,128)(2,1)S(1)}, u32[]{:S(2)}, u32[]{:S(2)}) %collective-permute-start.1) | collective-permute-done | bytes 524320 | tf_op jit(solution)/shard_map/ppermute | solution.py:56
  72.0 0.6 shard_map.81
  72.7 11.2 %all_to_all.34.blocks = bf16[4,64,1024]{2,1,0:T(8,128)(2,1)S(1)} all-to-all(bf16[4,64,1024]{2,1,0:T(8,128)(2,1)S(1)} %bitcast.13), channel_id=1, replica_groups={{48,32,16,0},{49,33,17,1},{50,34,18,2},{51,35,19,3},{52,36,20,4},{53,37..., dimensions={0} | all-to-all | bytes 1048576 | tf_op jit(solution)/shard_map/all_to_all | solution.py:41
  83.9 0.7 shard_map.82.after
  84.6 11.9 %all-to-all-start.5 = ((bf16[8,8,1024]{2,1,0:T(8,128)(2,1)}), bf16[8,8,1024]{2,1,0:T(8,128)(2,1)S(1)}, u32[]{:S(2)}, u32[]{:S(2)}) async-start(bf16[8,8,1024]{2,1,0:T(8,128)(2,1)} %bitcast.3), calls=%async_computation.5 | async-start | bytes 262144 | tf_op jit(solution)/shard_map/all_to_all | solution.py:41
  96.5 0.1 shard_map.83
  96.6 1.4 %convolution_convert_fusion = bf16[1024,512]{1,0:T(8,128)(2,1)} fusion(bf16[256,1024]{1,0:T(8,128)(2,1)S(1)} %get-tuple-element.10, bf16[256,512]{1,0:T(8,128)(2,1)S(1)} %get-tuple-element.11), kind=kOutput, calls=%fused_computation | convolution fusion | flops 268959744 | bytes 1835008 | tf_op jit(solution)/shard_map/dot_general | solution.py:37
  98.1 1.4 %convolution_convert_fusion.1 = bf16[512,1024]{1,0:T(8,128)(2,1)} fusion(bf16[256,512]{1,0:T(8,128)(2,1)S(1)} %get-tuple-element.8, bf16[256,1024]{1,0:T(8,128)(2,1)S(1)} %get-tuple-element.9), kind=kOutput, calls=%fused_computation.1 | convolution fusion | flops 268959744 | bytes 1835008 | tf_op jit(solution)/shard_map/dot_general | solution.py:37
  99.5 4.0 %all-to-all-done.5 = bf16[8,8,1024]{2,1,0:T(8,128)(2,1)S(1)} async-done(((bf16[8,8,1024]{2,1,0:T(8,128)(2,1)}), bf16[8,8,1024]{2,1,0:T(8,128)(2,1)S(1)}, u32[]{:S(2)}, u32[]{:S(2)}) %all-to-all-start.5) | async-done | bytes 131104 | tf_op jit(solution)/shard_map/all_to_all | solution.py:41
  103.5 0.6 fusion.1
  (3 shorter events, 0.1 us)
Async XLA Ops:
  1.3 33.5 %copy-start = (bf16[512,1024]{1,0:T(8,128)(2,1)S(1)}, bf16[512,1024]{1,0:T(8,128)(2,1)}, u32[]{:S(2)}) copy-start(bf16[512,1024]{1,0:T(8,128)(2,1)} %w_up.7) | copy-start | bytes 3145732
  1.4 33.5 %copy-start.1 = (bf16[1024,512]{1,0:T(8,128)(2,1)S(1)}, bf16[1024,512]{1,0:T(8,128)(2,1)}, u32[]{:S(2)}) copy-start(bf16[1024,512]{1,0:T(8,128)(2,1)} %w_down.7) | copy-start | bytes 3145732
  35.5 4.6 %collective-permute-start = (f32[8,32,1024]{2,1,0:T(8,128)S(1)}, f32[8,32,1024]{2,1,0:T(8,128)S(1)}, u32[]{:S(2)}, u32[]{:S(2)}) collective-permute-start(f32[8,32,1024]{2,1,0:T(8,128)S(1)} %shard_map.77), channel_id=1, source_target_pairs={{0,1},{1,0},{2,3},{3,2},{4,5},{5,4},{6,7},{7,6},{8,9},{9,8},{10,11... | collective-permute-start | bytes 3145736 | tf_op jit(solution)/shard_map/ppermute | solution.py:56
  68.3 3.8 %collective-permute-start.1 = (bf16[8,32,1024]{2,1,0:T(8,128)(2,1)S(1)}, bf16[8,32,1024]{2,1,0:T(8,128)(2,1)S(1)}, u32[]{:S(2)}, u32[]{:S(2)}) collective-permute-start(bf16[8,32,1024]{2,1,0:T(8,128)(2,1)S(1)} %all_to_all.33.half), channel_id=1, source_target_pairs={{0,1},{1,0},{2,3},{3,2},{4,5},{5,4},{6,7},{7,6},{8,9},{9,8},{10,11... | collective-permute-start | bytes 1572872 | tf_op jit(solution)/shard_map/ppermute | solution.py:56
  84.6 18.9 %all-to-all-start.5 = ((bf16[8,8,1024]{2,1,0:T(8,128)(2,1)}), bf16[8,8,1024]{2,1,0:T(8,128)(2,1)S(1)}, u32[]{:S(2)}, u32[]{:S(2)}) async-start(bf16[8,8,1024]{2,1,0:T(8,128)(2,1)} %bitcast.3), calls=%async_computation.5 | async-start | bytes 262144 | tf_op jit(solution)/shard_map/all_to_all | solution.py:41
